TPU v7x, 32 devices: a whole 2x2x4 slice. The times are simulated.
32 devices in a mesh: group: 1, expert: 16 (over z, y, x), seq: 2 (over core).
Axes of the slice: x: 2, y: 2, z: 4, core: 2. Of those that a mesh axis runs over, the one named last changes fastest.
Arguments:
- tokens: bfloat16 [2, 4096, 1664], P(('group', 'seq'), 'expert'), may hold values from -6 to 6
- router_w: bfloat16 [1664, 4], replicated, may hold values from -0.15625 to 0.15625
- expert_ids: int32 [2, 4096, 2], P(('group', 'seq'), 'expert'), may hold values from 0 to 3, all different within a row; in each aligned block of 256 rows (0 to 255, 256 to 511, ..., all dimensions but the last counted through in order) at most 256 rows name the same one
- w_in: bfloat16 [16, 1664, 2048], P('expert', None, 'seq'), may hold values from -0.15625 to 0.15625
- w_out: bfloat16 [16, 2048, 1664], P('expert', 'seq'), may hold values from -0.0625 to 0.0625
- w_qkv: bfloat16 [3, 1664, 832], P(None, None, 'seq'), may hold values from -0.15625 to 0.15625
Outputs:
- mixed: bfloat16 [2, 4096, 1664], P(('group', 'seq'), 'expert')
- attended: bfloat16 [2, 4096, 832], P('group', 'expert', 'seq')
Inputs may be any that keep to these rules, and one draw needn't show every extreme that they name: `expert_ids`: in each aligned block of 256 tokens (the tokens of one device, images taken in order) no expert is named by more than 256 of the choices, and this bound is reached; the two experts of a token differ.
All inputs are finite; a program needn't handle non-finite values.
Results may differ from a plain program's by a relative error of at most 0.019.
Values may be sent and summed in bfloat16 or wider, within the bound.
A program may use at most 192 MiB of HBM per device.

v0:
```python
import math

import jax
import jax.numpy as jnp
from jax import lax
from jax.sharding import PartitionSpec as P

HD = 104
SPLIT = 4


def layer_norm(values):
    values = values.astype(jnp.float32)
    center = jnp.mean(values, axis=-1, keepdims=True)
    spread = jnp.mean(jnp.square(values - center), axis=-1, keepdims=True)
    return ((values - center) * lax.rsqrt(spread + 1e-06)).astype(jnp.bfloat16)


def combine_pairs(merged, slot_index, keep_float, first_gate, second_gate, row_count):
    columns = merged.shape[-1]
    picked = jnp.take(merged, jnp.maximum(slot_index, 0), axis=0) * keep_float[:, None]
    picked = picked.reshape(row_count, 2, columns)
    return first_gate[:, None] * picked[:, 0] + second_gate[:, None] * picked[:, 1]


def shards(tokens, router_w, expert_ids, w_in, w_out, w_qkv):
    row_count = tokens.shape[1]
    width = tokens.shape[2]
    experts = router_w.shape[1]
    slots = max(2, 3 * row_count // experts)
    own_tokens = tokens[0]
    own_ids = expert_ids[0]
    normed = layer_norm(own_tokens)
    logits = jnp.dot(normed, router_w, preferred_element_type=jnp.float32)
    expert_range = jnp.arange(experts, dtype=jnp.int32)
    first_pick = jnp.sum(jnp.where(own_ids[:, 0:1] == expert_range[None, :], logits, 0.0), axis=1)
    second_pick = jnp.sum(jnp.where(own_ids[:, 1:2] == expert_range[None, :], logits, 0.0), axis=1)
    first_gate = jax.nn.sigmoid(first_pick - second_pick)
    second_gate = jax.nn.sigmoid(second_pick - first_pick)
    pair_ids = own_ids.reshape(row_count * 2)
    onehot = (pair_ids[:, None] == expert_range[None, :]).astype(jnp.int32)
    before = jnp.cumsum(onehot, axis=0) - onehot
    position = jnp.sum(before * onehot, axis=1)
    keeping = position < slots
    keep_float = keeping.astype(jnp.float32)
    slot_index = jnp.where(keeping, pair_ids * slots + position, -1)
    select = (slot_index[None, :] == jnp.arange(experts * slots, dtype=jnp.int32)[:, None]).astype(
        jnp.bfloat16
    )
    pair_rows = jnp.repeat(normed, 2, axis=0)
    packed = jnp.dot(select, pair_rows, preferred_element_type=jnp.float32).astype(jnp.bfloat16)
    outgoing = jnp.repeat(packed.reshape(experts, slots, width), SPLIT, axis=0)
    received = lax.all_to_all(outgoing, "expert", split_axis=0, concat_axis=0, tiled=True)
    w_first = w_in[0]
    w_second = w_out[0]
    piece = lax.all_gather(received, "seq", axis=1, tiled=True)
    sources = piece.shape[0]
    count = piece.shape[1]
    stacked = piece.reshape(sources * count, width)
    hidden = jax.nn.gelu(jnp.dot(stacked, w_first, preferred_element_type=jnp.float32)).astype(
        jnp.bfloat16
    )
    partial_value = jnp.dot(hidden, w_second, preferred_element_type=jnp.float32).reshape(
        sources, count, width
    )
    cores = partial_value.shape[1] // slots
    returned = lax.all_to_all(partial_value, "expert", split_axis=0, concat_axis=0, tiled=True)
    summed = jnp.sum(returned.reshape(experts, SPLIT, cores, slots, width), axis=1)
    own_part = lax.psum_scatter(summed, "seq", scatter_dimension=1, tiled=True)
    merged = own_part.reshape(experts * slots, width)
    combined = combine_pairs(merged, slot_index, keep_float, first_gate, second_gate, row_count)
    mixed = (own_tokens.astype(jnp.float32) + combined).astype(jnp.bfloat16)
    attn_local = layer_norm(mixed)
    attn_in = lax.all_gather(attn_local[None], "seq", axis=0, tiled=True)
    images = attn_in.shape[0]
    proj = jnp.einsum("ird,cdf->cirf", attn_in, w_qkv, preferred_element_type=jnp.float32).astype(
        jnp.bfloat16
    )
    head_cols = proj.shape[3]
    heads = head_cols // HD
    scale = 1.0 / math.sqrt(HD)
    queries = proj[0].reshape(images, row_count, heads, HD)
    key_vals = proj[1:3]
    piece = lax.all_gather(key_vals, "expert", axis=2, tiled=True)
    key_count = piece.shape[2]
    keys = piece[0].reshape(images, key_count, heads, HD)
    values = piece[1].reshape(images, key_count, heads, HD)
    scores = (
        jnp.einsum("iqhd,ikhd->ihqk", queries, keys, preferred_element_type=jnp.float32) * scale
    )
    weights = jnp.exp(scores)
    totals = jnp.sum(weights, axis=3)
    numerator = jnp.einsum(
        "ihqk,ikhd->ihqd", weights.astype(jnp.bfloat16), values, preferred_element_type=jnp.float32
    )
    numerator, totals = (numerator, totals)
    result = (numerator / totals[:, :, :, None]).astype(jnp.bfloat16)
    attended = jnp.transpose(result, (0, 2, 1, 3)).reshape(images, row_count, head_cols)
    return (mixed[None], attended)


def solution(mesh):
    in_specs = (
        P(("group", "seq"), "expert", None),
        P(),
        P(("group", "seq"), "expert", None),
        P("expert", None, "seq"),
        P("expert", "seq", None),
        P(None, None, "seq"),
    )
    out_specs = (P(("group", "seq"), "expert", None), P("group", "expert", "seq"))
    return jax.shard_map(shards, mesh=mesh, in_specs=in_specs, out_specs=out_specs, check_vma=False)
```

profile of v0, /device:TPU:0, one launch (start us, length us, event | category | flops | bytes accessed | tf_op | source)
XLA Modules:
  0.0 1599.8 jit_solution(7077823352974775410)
XLA Ops:
  7.2 1.0 copy.27
  8.2 0.7 eq.76
  9.1 1.4 convert_reduce_fusion
  10.4 1.5 fusion.25
  12.0 0.6 add_rsqrt_fusion.1
  12.5 1.2 reduce-window.6
  13.8 0.2 slice_reduce_fusion.2
  14.0 0.2 reduce-window.9
  14.2 0.7 fusion.57
  14.9 0.7 add_select_fusion
  15.6 1.4 fusion.26
  17.1 0.9 copy-done.3
  18.0 2.1 broadcast_in_dim.48
  20.0 4.7 reshape.242
  24.8 4.5 convolution_convert_fusion
  29.3 6.7 broadcast_in_dim.49
  36.0 231.9 %all_to_all.10 = bf16[16,192,1664]{2,1,0:T(8,128)(2,1)} all-to-all(bf16[16,192,1664]{2,1,0:T(8,128)(2,1)} %bitcast.127), channel_id=1, replica_groups=mesh['group'=1,'expert'=16,'seq'=2] {'expert'}, dimensions={0} | all-to-all | bytes 20447232 | tf_op jit(solution)/shard_map/all_to_all | solution.py:53
  268.0 0.2 all-reduce.3.cloned.1.call-start
  268.2 32.4 %all-gather.4.cloned.1.call-done = bf16[16,384,1664]{2,1,0:T(8,128)(2,1)} async-done(((bf16[16,192,1664]{2,1,0:T(8,128)(2,1)}), bf16[16,384,1664]{2,1,0:T(8,128)(2,1)}) %all-gather.4.cloned.1.call-update) | async-done | bytes 20447248 | tf_op jit(solution)/shard_map/all_gather | solution.py:56
  300.6 31.7 %fusion.9 = bf16[6144,1024]{1,0:T(8,128)(2,1)S(1)} fusion(bf16[6144,1664]{1,0:T(8,128)(2,1)} %bitcast.136, bf16[1,1664,1024]{2,1,0:T(8,128)(2,1)} %param.9), kind=kOutput, calls=%fused_computation.12 | convolution fusion | flops 20994588672 | bytes 36438016 | tf_op jit(solution)/shard_map/dot_general | solution.py:60
  332.3 27.7 %fusion.15 = f32[16,384,1664]{2,1,0:T(8,128)} fusion(bf16[16,384,1024]{2,1,0:T(8,128)(2,1)S(1)} %bitcast.137, bf16[1,1024,1664]{2,1,0:T(8,128)(2,1)S(1)} %copy-done), kind=kOutput, calls=%fused_computation.17 | convolution fusion | flops 20937965568 | bytes 56885248 | tf_op jit(solution)/shard_map/dot_general | solution.py:63
  360.0 889.2 %all_to_all.11 = f32[16,384,1664]{2,1,0:T(8,128)} all-to-all(f32[16,384,1664]{2,1,0:T(8,128)} %fusion.15), channel_id=1, replica_groups=mesh['group'=1,'expert'=16,'seq'=2] {'expert'}, dimensions={0} | all-to-all | bytes 81788928 | tf_op jit(solution)/shard_map/all_to_all | solution.py:67
  1249.2 22.5 %reduce_sum.91 = f32[4,2,192,1664]{3,2,1,0:T(8,128)} reduce(f32[4,4,2,192,1664]{4,3,2,1,0:T(8,128)} %bitcast.124, f32[]{:T(128)} %constant.17.clone.1), dimensions={1}, to_apply=%region_7.8 | reduce | flops 7667712 | bytes 51118084 | tf_op jit(solution)/shard_map/reduce_sum | solution.py:68
  1271.7 0.3 all-gather.6.cloned.1.call-start
  1272.0 0.1 reduce_sum.90
  1272.2 0.2 copy-done.8
  1272.5 0.1 mul.134
  1272.7 0.6 dynamic-slice
  1273.3 0.2 slice_reduce_fusion.1
  1273.5 0.4 select_reduce_fusion.1
  1273.9 0.7 fusion.54
  1274.6 38.4 %all-reduce.3.cloned.1.call-done = f32[4,2,192,1664]{3,2,1,0:T(8,128)} async-done(((f32[4,2,192,1664]{3,2,1,0:T(8,128)}), f32[4,2,192,1664]{3,2,1,0:T(8,128)}) %all-reduce.3.cloned.1.call-update) | async-done | bytes 10223632
  1313.0 5.7 constant_dynamic-slice_fusion
  1318.7 7.2 gather_fusion
  1325.9 4.0 gather.7
  1329.9 3.0 select_multiply_fusion
  1333.0 2.6 fusion.64
  1335.6 0.5 convert_reduce_fusion.1
  1336.1 0.4 fusion.28
  1336.5 1.7 multiply_convert_fusion
  1338.3 0.3 all-gather.8.cloned.1.call-start
  1338.6 11.0 all-gather.6.cloned.1.call-done
  1349.6 5.2 fusion.39
  1354.8 1.0 slice.48
  1355.9 199.0 %all-gather.8.cloned.1.call-done = bf16[2,2,4096,416]{2,3,0,1:T(8,128)(2,1)} async-done(((bf16[2,2,256,416]{2,3,0,1:T(8,128)(2,1)}), bf16[2,2,4096,416]{2,3,0,1:T(8,128)(2,1)}) %all-gather.8.cloned.1.call-update) | async-done | bytes 13631504 | tf_op jit(solution)/shard_map/all_gather | solution.py:84
  1554.8 8.2 fusion.63
  1563.1 13.7 fusion
  1576.7 16.5 %fusion.50 = bf16[2,256,4,104]{1,3,2,0:T(8,128)(2,1)} fusion(bf16[2,4096,4,104]{1,3,2,0:T(8,128)(2,1)} %bitcast.125, f32[2,4,256,4096]{3,2,1,0:T(8,128)} %get-tuple-element.19, f32[2,256,4]{1,2,0:T(4,128)S(1)} %bitcast.132), kind=kOutput, calls=%fused_computation.51 | convolution fusion | flops 1762033664 | bytes 40804352 | tf_op jit(solution)/shard_map/ihqk,ikhd->ihqd/dot_general | solution.py:93
  (35 shorter events, 0.6 us)
Async XLA Ops:
  7.2 325.1 %copy-start = (bf16[1,1024,1664]{2,1,0:T(8,128)(2,1)S(1)}, bf16[1,1024,1664]{2,1,0:T(8,128)(2,1)}, u32[]{:S(2)}) copy-start(bf16[1,1024,1664]{2,1,0:T(8,128)(2,1)} %param.10) | copy-start | bytes 10223620
  7.2 293.4 %all-gather.4.cloned.1.call-start = ((), (), s32[]{:S(2)}) async-start(), calls=%async_computation.2 | async-start | bytes 30670848 | tf_op jit(solution)/shard_map/all_gather | solution.py:56
  10.4 2.1 copy-start.7
  17.1 0.9 copy-start.3
  268.0 1045.1 %all-reduce.3.cloned.1.call-start = ((), (), s32[]{:S(2)}) async-start(), calls=%async_computation.5 | async-start | bytes 20447232
  1271.7 0.7 copy-start.8
  1271.7 1.0 copy-start.9
  1271.7 1.8 copy-start.4
  1271.7 1.8 copy-start.6
  1271.7 77.9 %all-gather.6.cloned.1.call-start = ((), (), s32[]{:S(2)}) async-start(), calls=%async_computation.3 | async-start | bytes 2555904 | tf_op jit(solution)/shard_map/all_gather | solution.py:74
  1325.9 4.0 copy-start.5
  1332.9 2.7 copy-start.2
  1338.3 216.6 %all-gather.8.cloned.1.call-start = ((), (), s32[]{:S(2)}) async-start(), calls=%async_computation.4 | async-start | bytes 14483456 | tf_op jit(solution)/shard_map/all_gather | solution.py:84
  1576.7 16.5 %copy-start.1 = (bf16[1,1024,1664]{2,1,0:T(8,128)(2,1)S(1)}, bf16[1,1024,1664]{2,1,0:T(8,128)(2,1)}, u32[]{:S(2)}) copy-start(bf16[1,1024,1664]{2,1,0:T(8,128)(2,1)} %param.10) | copy-start | bytes 10223620
Sparse Core Ops, SparseCore 0:
  268.1 32.4 all-gather.3
  1271.9 41.1 all-reduce.2
  1338.4 11.1 all-gather.5
  1355.9 198.8 all-gather.7
where the time goes:
time: 1600 us
  blocking collectives  1120 us (70%)
  waiting for transfers between devices  281 us (18%)
  matrix products  99.6 us (6%)
  local copies, waits for them, and re-layouts  46.6 us (3%)
  other arithmetic  36.7 us (2%)
    all_to_all x1, blocking collectives, shards(): lax.all_to_all(partial_value, 'expert', split_axis=0, concat_axis=0, tile...  889 us
    all_to_all x1, blocking collectives, shards(): lax.all_to_all(outgoing, 'expert', split_axis=0, concat_axis=0, tiled=True)  232 us
    all_gather x1, waiting for transfers between devices, shards(): piece = lax.all_gather(key_vals, 'expert', axis=2, tiled=True)  199 us
    unnamed x5, waiting for transfers between devices  38.5 us
    all_gather x1, waiting for transfers between devices, shards(): piece = lax.all_gather(received, 'seq', axis=1, tiled=True)  32.4 us
  transfers between devices with their start and end apart: 4, of which 4 were waited for; matrix products, arithmetic and copies ran while one was open for 0% of the time, Pallas kernels for 0%

commit v1 on v0

v1 whole, which is shorter than its diff:
```python
import functools
import math

import jax
import jax.numpy as jnp
from jax import lax
from jax.experimental import pallas as pl
from jax.experimental.pallas import tpu as pltpu
from jax.sharding import PartitionSpec as P

HD = 104
SPLIT = 4
MIB = 1024 * 1024


def layer_norm(values):
    values = values.astype(jnp.float32)
    center = jnp.mean(values, axis=-1, keepdims=True)
    spread = jnp.mean(jnp.square(values - center), axis=-1, keepdims=True)
    return ((values - center) * lax.rsqrt(spread + 1e-06)).astype(jnp.bfloat16)


def gelu(value):
    inner = math.sqrt(2.0 / math.pi) * (value + 0.044715 * value * value * value)
    return 0.5 * value * (1.0 + jnp.tanh(inner))


def mlp_kernel(steps, chunk, has_base, rows_ref, *refs):
    w_in_refs, w_out_refs = refs[0:2], refs[2:4]
    base_ref = refs[4] if has_base else None
    out_ref, acc_ref = refs[-2], refs[-1]
    j = pl.program_id(0)
    count = rows_ref.shape[0]

    @pl.when(j == 0)
    def _():
        if has_base:
            acc_ref[...] = base_ref[...].astype(jnp.float32)
        else:
            acc_ref[...] = jnp.zeros_like(acc_ref)

    for block in range(2):

        @pl.when(j // steps == block)
        def _():
            for start in range(0, count, chunk):
                part = pl.ds(start, chunk)
                up = jnp.dot(
                    rows_ref[part, :], w_in_refs[block][...], preferred_element_type=jnp.float32
                )
                hidden = gelu(up).astype(jnp.bfloat16)
                acc_ref[part, :] += jnp.dot(
                    hidden, w_out_refs[block][...], preferred_element_type=jnp.float32
                )

    @pl.when(j == 2 * steps - 1)
    def _():
        out_ref[...] = acc_ref[...].astype(out_ref.dtype)


def mlp(rows, w_ins, w_outs, base, out_dtype):
    count, width = rows.shape
    units = w_ins[0].shape[1]
    tile = 512 if units % 512 == 0 else units
    steps = units // tile
    chunk = 256 if count % 256 == 0 else count

    def in_map(block):
        return lambda j: (0, jnp.clip(j - block * steps, 0, steps - 1))

    def out_map(block):
        return lambda j: (jnp.clip(j - block * steps, 0, steps - 1), 0)

    whole = pl.BlockSpec((count, width), lambda j: (0, 0))
    in_specs = [whole]
    in_specs += [pl.BlockSpec((width, tile), in_map(b)) for b in range(2)]
    in_specs += [pl.BlockSpec((tile, width), out_map(b)) for b in range(2)]
    operands = [rows, *w_ins, *w_outs]
    if base is not None:
        in_specs.append(whole)
        operands.append(base)
    return pl.pallas_call(
        functools.partial(mlp_kernel, steps, chunk, base is not None),
        grid=(2 * steps,),
        out_shape=jax.ShapeDtypeStruct((count, width), out_dtype),
        in_specs=in_specs,
        out_specs=whole,
        scratch_shapes=[pltpu.VMEM((count, width), jnp.float32)],
        compiler_params=pltpu.CompilerParams(
            vmem_limit_bytes=56 * MIB, dimension_semantics=("arbitrary",)
        ),
        cost_estimate=pl.CostEstimate(
            flops=8 * count * width * units,
            bytes_accessed=8 * width * units + 10 * count * width,
            transcendentals=2 * count * units,
        ),
    )(*operands)


def attention_kernel(key_tile, q_ref, k_ref, v_ref, out_ref):
    queries = q_ref[...]
    factor = math.log2(math.e) / math.sqrt(HD)
    width = queries.shape[1]
    total = jnp.zeros((1, width), jnp.float32)
    summed = jnp.zeros((HD, width), jnp.float32)
    for start in range(0, k_ref.shape[0], key_tile):
        part = pl.ds(start, key_tile)
        scores = jnp.dot(k_ref[part, :], queries, preferred_element_type=jnp.float32)
        weights = jnp.exp2(scores * factor)
        total += jnp.sum(weights, axis=0, keepdims=True)
        summed += jnp.dot(
            v_ref[:, part], weights.astype(jnp.bfloat16), preferred_element_type=jnp.float32
        )
    out_ref[...] = (summed / total).astype(out_ref.dtype)


def attention(queries, keys, values):
    columns = queries.shape[1]
    key_count = keys.shape[0]
    tile = 512 if columns % 512 == 0 else columns
    key_tile = 512 if key_count % 512 == 0 else key_count
    return pl.pallas_call(
        functools.partial(attention_kernel, key_tile),
        grid=(columns // tile,),
        out_shape=jax.ShapeDtypeStruct((HD, columns), jnp.bfloat16),
        in_specs=[
            pl.BlockSpec((HD, tile), lambda j: (0, j)),
            pl.BlockSpec((key_count, HD), lambda j: (0, 0)),
            pl.BlockSpec((HD, key_count), lambda j: (0, 0)),
        ],
        out_specs=pl.BlockSpec((HD, tile), lambda j: (0, j)),
        compiler_params=pltpu.CompilerParams(
            vmem_limit_bytes=48 * MIB, dimension_semantics=("arbitrary",)
        ),
        cost_estimate=pl.CostEstimate(
            flops=4 * HD * columns * key_count,
            bytes_accessed=4 * HD * (columns + key_count),
            transcendentals=columns * key_count,
        ),
    )(queries, keys, values)


def shards(places, tokens, router_w, expert_ids, w_in, w_out, w_qkv):
    row_count = tokens.shape[1]
    width = tokens.shape[2]
    experts = router_w.shape[1]
    slots = max(2, 3 * row_count // experts)
    columns = [[e * SPLIT + q for e in range(experts)] for q in range(SPLIT)]

    def across(value, bit):
        return lax.ppermute(value, "expert", [(p, p ^ bit) for p in range(places)])

    def other_core(value):
        return lax.ppermute(value, "seq", [(0, 1), (1, 0)])

    own_weights = (w_in[0], w_out[0])
    core_weights = tuple(other_core(w) for w in own_weights)
    far_weights = tuple(across(w, 1) for w in own_weights)
    far_core_weights = tuple(other_core(w) for w in far_weights)

    own_tokens = tokens[0]
    own_ids = expert_ids[0]
    normed = layer_norm(own_tokens)
    logits = jnp.dot(normed, router_w, preferred_element_type=jnp.float32)
    expert_range = jnp.arange(experts, dtype=jnp.int32)
    first_pick = jnp.sum(jnp.where(own_ids[:, 0:1] == expert_range[None, :], logits, 0.0), axis=1)
    second_pick = jnp.sum(jnp.where(own_ids[:, 1:2] == expert_range[None, :], logits, 0.0), axis=1)
    first_gate = jax.nn.sigmoid(first_pick - second_pick)
    second_gate = jax.nn.sigmoid(second_pick - first_pick)
    pair_ids = own_ids.reshape(row_count * 2)
    onehot = (pair_ids[:, None] == expert_range[None, :]).astype(jnp.int32)
    before = jnp.cumsum(onehot, axis=0) - onehot
    position = jnp.sum(before * onehot, axis=1)
    slot_index = jnp.where(position < slots, pair_ids * slots + position, -1)
    slot_index = slot_index.reshape(row_count, 2)
    slot_range = jnp.arange(experts * slots, dtype=jnp.int32)
    is_first = slot_index[:, 0:1] == slot_range[None, :]
    is_second = slot_index[:, 1:2] == slot_range[None, :]
    select = (is_first | is_second).astype(jnp.bfloat16)
    packed = lax.dot_general(
        select, normed, (((0,), (0,)), ((), ())), preferred_element_type=jnp.float32
    ).astype(jnp.bfloat16)
    outgoing = packed.reshape(experts, slots, width)
    received = lax.all_to_all(
        outgoing, "expert", split_axis=0, concat_axis=0, tiled=True, axis_index_groups=columns
    )
    near_rows = received.reshape(experts * slots, width)
    far_rows = across(near_rows, 2)

    chip_in, chip_out = zip(own_weights, core_weights)
    next_in, next_out = zip(far_weights, far_core_weights)
    near_sum = mlp(near_rows, chip_in, chip_out, None, jnp.float32)
    far_sum = mlp(far_rows, chip_in, chip_out, None, jnp.float32)
    far_sum = mlp(far_rows, next_in, next_out, far_sum, jnp.bfloat16)
    arrived = across(far_sum, 2)
    near_sum = mlp(near_rows, next_in, next_out, near_sum, jnp.float32)
    summed = (near_sum + arrived.astype(jnp.float32)).astype(jnp.bfloat16)
    merged = lax.all_to_all(
        summed.reshape(experts, slots, width),
        "expert",
        split_axis=0,
        concat_axis=0,
        tiled=True,
        axis_index_groups=columns,
    ).reshape(experts * slots, width)

    gates = jnp.where(is_first, first_gate[:, None], 0.0) + jnp.where(
        is_second, second_gate[:, None], 0.0
    )
    high = gates.astype(jnp.bfloat16)
    low = (gates - high.astype(jnp.float32)).astype(jnp.bfloat16)
    combined = jnp.dot(high, merged, preferred_element_type=jnp.float32) + jnp.dot(
        low, merged, preferred_element_type=jnp.float32
    )
    mixed = (own_tokens.astype(jnp.float32) + combined).astype(jnp.bfloat16)
    attn_local = layer_norm(mixed)
    attn_in = lax.all_gather(attn_local[None], "seq", axis=0, tiled=True)
    images = attn_in.shape[0]
    proj = jnp.einsum("cdf,ird->cifr", w_qkv, attn_in, preferred_element_type=jnp.float32).astype(
        jnp.bfloat16
    )
    heads = proj.shape[2] // HD
    pairs = images * heads
    share = places // pairs
    part = row_count // share
    proj = proj.reshape(3, pairs, HD, row_count)
    query_parts = proj[0].reshape(pairs, HD, share, part).transpose(0, 2, 1, 3)
    key_parts = jnp.broadcast_to(proj[1][:, None], (pairs, share, HD, row_count))
    value_parts = jnp.broadcast_to(proj[2][:, None], (pairs, share, HD, row_count))
    leaving = jnp.concatenate([key_parts, value_parts, query_parts], axis=3).reshape(
        places, HD, 2 * row_count + part
    )
    landed = lax.all_to_all(leaving, "expert", split_axis=0, concat_axis=0, tiled=True)
    keys = landed[:, :, :row_count].transpose(0, 2, 1).reshape(places * row_count, HD)
    values = landed[:, :, row_count : 2 * row_count].transpose(1, 0, 2)
    values = values.reshape(HD, places * row_count)
    queries = landed[:, :, 2 * row_count :].transpose(1, 0, 2).reshape(HD, places * part)
    result = attention(queries, keys, values)
    result = result.reshape(HD, places, part).transpose(1, 0, 2)
    returned = lax.all_to_all(result, "expert", split_axis=0, concat_axis=0, tiled=True)
    attended = returned.reshape(images, heads, share, HD, part).transpose(0, 2, 4, 1, 3)
    attended = attended.reshape(images, row_count, heads * HD)
    return (mixed[None], attended)


def solution(mesh):
    in_specs = (
        P(("group", "seq"), "expert", None),
        P(),
        P(("group", "seq"), "expert", None),
        P("expert", None, "seq"),
        P("expert", "seq", None),
        P(None, None, "seq"),
    )
    out_specs = (P(("group", "seq"), "expert", None), P("group", "expert", "seq"))
    return jax.shard_map(
        functools.partial(shards, mesh.shape["expert"]),
        mesh=mesh,
        in_specs=in_specs,
        out_specs=out_specs,
        check_vma=False,
    )
```

time: 1600 us -> 459 us (0.29)
  blocking collectives: 1120 us -> 73.4 us
  Pallas kernels: 0 us -> 96.8 us
  matrix products: 99.6 us -> 13.8 us
  waiting for transfers between devices: 281 us -> 223 us
  local copies, waits for them, and re-layouts: 46.6 us -> 9.98 us
  other arithmetic: 36.7 us -> 10.5 us
    all_to_all x2, blocking collectives: 1120 us -> 73.4 us  [the longest x1 57.6 us: shards(): lax.all_to_all(leaving, 'expert', split_axis=0, concat_axis=0, tiled=True)]
    all_gather x2 -> x0, waiting for transfers between devices: 231 us -> none  [the longest x1 199 us: shards(): piece = lax.all_gather(key_vals, 'expert', axis=2, tiled=True)]
    all_to_all x0 -> x2, waiting for transfers between devices: none -> 112 us  [the longest x1 56.5 us: shards(): lax.all_to_all(summed.reshape(experts, slots, width), 'expert', split_axi...]
    ppermute x0 -> x8, waiting for transfers between devices: none -> 102 us  [the longest x4 102 us: across(): return lax.ppermute(value, 'expert', [(p, p ^ bit) for p in range(places)])]
    pallas_call x0 -> x5, Pallas kernels: none -> 96.8 us  [the longest x4 86.1 us: mlp(): pl.pallas_call(functools.partial(mlp_kernel, steps, chunk, base is not No...]
    dot_general x6 -> x4, matrix products: 99.3 us -> 12.7 us  [the longest x1 5.21 us: shards(): jnp.einsum('cdf,ird->cifr', w_qkv, attn_in, preferred_element_type=jnp.fl...]
    unnamed x5 -> x1, waiting for transfers between devices: 38.5 us -> 0.02 us
    reduce_sum x1 -> x0, other arithmetic: 22.5 us -> none  [shards(): jnp.sum(returned.reshape(experts, SPLIT, cores, slots, width), axis=1)]
  transfers between devices with their start and end apart: 4 -> 11, of which waited for: 4 -> 6; matrix products, arithmetic and copies ran while one was open for 0% -> 0% of each run, Pallas kernels for 0% -> 14%
where the time goes in v1:
time: 459 us
  waiting for transfers between devices  223 us (49%)
  Pallas kernels  96.8 us (21%)
  blocking collectives  73.4 us (16%)
  starting transfers between devices  16.7 us (4%)
  between operations  14.4 us (3%)
  matrix products  13.8 us (3%)
  other arithmetic  10.5 us (2%)
  local copies, waits for them, and re-layouts  9.98 us (2%)
    ppermute x4, waiting for transfers between devices, across(): return lax.ppermute(value, 'expert', [(p, p ^ bit) for p in range(places)])  102 us
    pallas_call x4, Pallas kernels, mlp(): pl.pallas_call(functools.partial(mlp_kernel, steps, chunk, base is not No...  86.1 us
    all_to_all x1, blocking collectives, shards(): lax.all_to_all(leaving, 'expert', split_axis=0, concat_axis=0, tiled=True)  57.6 us
    all_to_all x1, waiting for transfers between devices, shards(): lax.all_to_all(summed.reshape(experts, slots, width), 'expert', split_axi...  56.5 us
    all_to_all x1, waiting for transfers between devices, shards(): lax.all_to_all(outgoing, 'expert', split_axis=0, concat_axis=0, tiled=Tru...  55.5 us
    all_to_all x1, blocking collectives, shards(): lax.all_to_all(result, 'expert', split_axis=0, concat_axis=0, tiled=True)  15.8 us
    pallas_call x1, Pallas kernels, attention(): pl.pallas_call(functools.partial(attention_kernel, key_tile), grid=(colum...  10.6 us
    all_gather x1, waiting for transfers between devices, shards(): attn_in = lax.all_gather(attn_local[None], 'seq', axis=0, tiled=True)  9.26 us
  transfers between devices with their start and end apart: 11, of which 6 were waited for; matrix products, arithmetic and copies ran while one was open for 0% of the time, Pallas kernels for 14%

profile of v1, /device:TPU:0, one launch (start us, length us, event | category | flops | bytes accessed | tf_op | source)
XLA Modules:
  0.0 458.8 jit_solution(14802649665573472404)
XLA Ops:
  7.2 0.9 copy.29
  8.1 0.1 eq.89
  8.2 0.1 eq.85
  8.4 1.4 convert_reduce_fusion.1
  9.7 1.5 fusion.11
  11.3 1.2 reduce-window.6
  12.5 0.2 slice_reduce_fusion.4
  12.7 0.2 reduce-window.9
  13.0 0.1 reduce_sum.66
  13.2 0.2 slice_reduce_fusion.3
  13.4 2.7 convolution_convert_fusion
  16.2 6.3 %all-to-all-start = ((bf16[4,192,1664]{2,1,0:T(8,128)(2,1)}), bf16[4,192,1664]{2,1,0:T(8,128)(2,1)S(1)}, u32[]{:S(2)}, u32[]{:S(2)}) async-start(bf16[4,192,1664]{2,1,0:T(8,128)(2,1)} %bitcast.107), calls=%async_computation | async-start | bytes 5111808 | tf_op jit(solution)/shard_map/all_to_all | solution.py:184
  22.5 1.5 collective-permute-start
  24.0 0.5 collective-permute-start.2
  24.5 0.5 collective-permute-start.5
  25.0 55.5 %all-to-all-done = bf16[4,192,1664]{2,1,0:T(8,128)(2,1)S(1)} async-done(((bf16[4,192,1664]{2,1,0:T(8,128)(2,1)}), bf16[4,192,1664]{2,1,0:T(8,128)(2,1)S(1)}, u32[]{:S(2)}, u32[]{:S(2)}) %all-to-all-start) | async-done | bytes 2555936 | tf_op jit(solution)/shard_map/all_to_all | solution.py:184
  80.5 1.5 collective-permute-start.6
  82.0 17.4 %collective-permute-done.refs_0_ = bf16[1664,1024]{1,0:T(8,128)(2,1)} collective-permute-done((bf16[1664,1024]{1,0:T(8,128)(2,1)}, bf16[1664,1024]{1,0:T(8,128)(2,1)}, u32[]{:S(2)}, u32[]{:S(2)}) %collective-permute-start) | collective-permute-done | bytes 3407904 | tf_op jit(solution)/shard_map/ppermute | solution.py:151
  99.5 71.6 %collective-permute-done.2.refs_2_ = bf16[1024,1664]{1,0:T(8,128)(2,1)} collective-permute-done((bf16[1024,1664]{1,0:T(8,128)(2,1)}, bf16[1024,1664]{1,0:T(8,128)(2,1)}, u32[]{:S(2)}, u32[]{:S(2)}) %collective-permute-start.2) | collective-permute-done | bytes 3407904 | tf_op jit(solution)/shard_map/ppermute | solution.py:151
  171.0 21.0 %shard_map.79.refs_4_ = f32[768,1664]{1,0:T(8,128)} custom-call(bf16[768,1664]{1,0:T(8,128)(2,1)} %collective-permute-done.6.rows_ref, bf16[1664,1024]{1,0:T(8,128)(2,1)} %bitcast.115, bf16[1664,1024]{1,0:T(8,128)(2,1)} %collective-permute-done.4.refs_1_, bf16[1024,1664]{1,0:T(8,128)(2,1)} %bitcast.119, bf16[1024,1664]{1,0:T(8,128)(2,1)} %collective-permute-done.5.refs_3_), custom_call_target="tpu_custom_call" | custom-call | flops 10468982784 | bytes 26411008 | tf_op jit(solution)/shard_map/pallas_call | solution.py:82
  192.1 1.7 copy-done.14
  193.8 21.5 %shard_map.80 = bf16[768,1664]{1,0:T(8,128)(2,1)} custom-call(bf16[768,1664]{1,0:T(8,128)(2,1)} %collective-permute-done.6.rows_ref, bf16[1664,1024]{1,0:T(8,128)(2,1)} %collective-permute-done.refs_0_, bf16[1664,1024]{1,0:T(8,128)(2,1)} %copy-done.14, bf16[1024,1664]{1,0:T(8,128)(2,1)} %collective-permute-done.2.refs_2_, ...), custom_call_target="tpu_custom_call" | custom-call | flops 10468982784 | bytes 26411008 | tf_op jit(solution)/shard_map/pallas_call | solution.py:82
  215.3 1.5 collective-permute-start.7
  216.8 21.1 %shard_map.77.refs_4_ = f32[768,1664]{1,0:T(8,128)} custom-call(bf16[768,1664]{1,0:T(8,128)(2,1)} %bitcast.103, bf16[1664,1024]{1,0:T(8,128)(2,1)} %bitcast.116, bf16[1664,1024]{1,0:T(8,128)(2,1)} %collective-permute-done.4.refs_1_, bf16[1024,1664]{1,0:T(8,128)(2,1)} %bitcast.120, bf16[1024,1664]{1,0:T(8,128)(2,1)} %collective-permute-done.5.refs_3_), custom_call_target="tpu_custom_call" | custom-call | flops 10468982784 | bytes 26411008 | tf_op jit(solution)/shard_map/pallas_call | solution.py:82
  237.9 22.5 %shard_map.78 = f32[768,1664]{1,0:T(8,128)} custom-call(bf16[768,1664]{1,0:T(8,128)(2,1)} %bitcast.104, bf16[1664,1024]{1,0:T(8,128)(2,1)} %collective-permute-done.refs_0_, bf16[1664,1024]{1,0:T(8,128)(2,1)} %copy-done.14, bf16[1024,1664]{1,0:T(8,128)(2,1)} %collective-permute-done.2.refs_2_, bf16[1024,1664]{1,0:T(8,128)(2,1)} %collective-permute-done.3.refs_3_, ...), custom_call_target="tpu_custom_call" | custom-call | flops 10468982784 | bytes 26411008 | tf_op jit(solution)/shard_map/pallas_call | solution.py:82
  260.4 13.0 %collective-permute-done.7 = bf16[768,1664]{1,0:T(8,128)(2,1)S(1)} collective-permute-done((bf16[768,1664]{1,0:T(8,128)(2,1)}, bf16[768,1664]{1,0:T(8,128)(2,1)S(1)}, u32[]{:S(2)}, u32[]{:S(2)}) %collective-permute-start.7) | collective-permute-done | bytes 2555936 | tf_op jit(solution)/shard_map/ppermute | solution.py:151
  273.4 4.4 add_convert_fusion
  277.8 4.8 %all-to-all-start.1 = ((bf16[4,192,1664]{2,1,0:T(8,128)(2,1)}), bf16[4,192,1664]{2,1,0:T(8,128)(2,1)S(1)}, u32[]{:S(2)}, u32[]{:S(2)}) async-start(bf16[4,192,1664]{2,1,0:T(8,128)(2,1)} %bitcast.7), calls=%async_computation.1 | async-start | bytes 5111808 | tf_op jit(solution)/shard_map/all_to_all | solution.py:198
  282.6 0.2 slice_reduce_fusion.2
  282.8 1.1 select_reduce_fusion.1
  284.0 56.5 %all-to-all-done.1 = bf16[4,192,1664]{2,1,0:T(8,128)(2,1)S(1)} async-done(((bf16[4,192,1664]{2,1,0:T(8,128)(2,1)}), bf16[4,192,1664]{2,1,0:T(8,128)(2,1)S(1)}, u32[]{:S(2)}, u32[]{:S(2)}) %all-to-all-start.1) | async-done | bytes 2555936 | tf_op jit(solution)/shard_map/all_to_all | solution.py:198
  340.5 1.5 copy-done.5
  342.0 1.8 fusion.22
  343.8 3.0 convert_reduce_fusion
  346.8 0.4 fusion.9
  347.2 1.2 fusion.10
  348.4 9.3 %all-gather.3.cloned.1.call-done = bf16[512,1664]{1,0:T(8,128)(2,1)} async-done(((bf16[256,1664]{1,0:T(8,128)(2,1)}), bf16[512,1664]{1,0:T(8,128)(2,1)}) %all-gather.3.cloned.1.call-update) | async-done | bytes 1703952 | tf_op jit(solution)/shard_map/all_gather | solution.py:217
  357.7 5.2 %fusion.16 = bf16[3,2,416,256]{3,2,0,1:T(8,128)(2,1)S(1)} fusion(bf16[2,256,1664,1]{2,1,3,0:T(8,128)(2,1)} %bitcast.121, bf16[3,1664,416]{1,2,0:T(8,128)(2,1)} %param.11), kind=kOutput, calls=%fused_computation.22 | convolution fusion | flops 2127151104 | bytes 7135232 | tf_op jit(solution)/shard_map/cdf,ird->cifr/dot_general | solution.py:219
  363.3 0.2 pad_maximum_fusion
  363.5 57.6 %all_to_all.20 = bf16[16,104,640]{2,1,0:T(8,128)(2,1)S(1)} all-to-all(bf16[16,104,640]{2,1,0:T(8,128)(2,1)S(1)} %bitcast.99), channel_id=1, replica_groups=mesh['group'=1,'expert'=16,'seq'=2] {'expert'}, dimensions={0} | all-to-all | bytes 4259840 | tf_op jit(solution)/shard_map/all_to_all | solution.py:233
  421.1 0.1 slice_bitcast_fusion
  421.3 1.2 copy-done.1
  422.4 0.6 copy.34
  423.1 1.0 copy_bitcast_fusion.q_ref
  424.1 10.6 %shard_map.81 = bf16[104,2048]{1,0:T(8,128)(2,1)S(1)} custom-call(bf16[104,2048]{1,0:T(8,128)(2,1)S(1)} %copy_bitcast_fusion.q_ref, bf16[4096,104]{1,0:T(8,128)(2,1)S(1)} %bitcast.97, bf16[104,4096]{1,0:T(8,128)(2,1)S(1)} %bitcast.98), custom_call_target="tpu_custom_call" | custom-call | flops 3489660928 | bytes 2555904 | tf_op jit(solution)/shard_map/pallas_call | solution.py:122
  434.8 15.8 %all_to_all.21 = bf16[16,104,128]{2,1,0:T(8,128)(2,1)S(1)} all-to-all(bf16[16,104,128]{2,1,0:T(8,128)(2,1)S(1)} %bitcast_bitcast_fusion), channel_id=1, replica_groups=mesh['group'=1,'expert'=16,'seq'=2] {'expert'}, dimensions={0} | all-to-all | bytes 851968 | tf_op jit(solution)/shard_map/all_to_all | solution.py:240
  450.6 0.3 copy.37
  450.9 1.0 reshape.120
  (53 shorter events, 0.8 us)
Async XLA Ops:
  7.2 275.6 %copy-start = (bf16[1664,4]{0,1:T(4,128)(2,1)S(1)}, bf16[1664,4]{0,1:T(4,128)(2,1)}, u32[]{:S(2)}) copy-start(bf16[1664,4]{0,1:T(4,128)(2,1)} %param.7) | copy-start | bytes 39940
  7.2 6.3 %copy-start.2 = (bf16[1,256,1664]{2,1,0:T(8,128)(2,1)S(1)}, bf16[1,256,1664]{2,1,0:T(8,128)(2,1)}, u32[]{:S(2)}) copy-start(bf16[1,256,1664]{2,1,0:T(8,128)(2,1)} %param.6) | copy-start | bytes 2555908
  9.7 6.4 %copy-start.6 = (f32[256]{0:T(256)}, f32[256]{0:T(256)S(1)}, u32[]{:S(2)}) copy-start(f32[256]{0:T(256)S(1)} %broadcast_multiply_fusion.1) | copy-start | bytes 3076
  11.3 4.9 %copy-start.11 = (f32[256]{0:T(256)}, f32[256]{0:T(256)S(1)}, u32[]{:S(2)}) copy-start(f32[256]{0:T(256)S(1)} %add_rsqrt_fusion.1) | copy-start | bytes 3076
  13.4 2.7 copy-start.7
  13.4 2.7 copy-start.9
  16.2 64.4 %all-to-all-start = ((bf16[4,192,1664]{2,1,0:T(8,128)(2,1)}), bf16[4,192,1664]{2,1,0:T(8,128)(2,1)S(1)}, u32[]{:S(2)}, u32[]{:S(2)}) async-start(bf16[4,192,1664]{2,1,0:T(8,128)(2,1)} %bitcast.107), calls=%async_computation | async-start | bytes 5111808 | tf_op jit(solution)/shard_map/all_to_all | solution.py:184
  22.5 77.0 %collective-permute-start = (bf16[1664,1024]{1,0:T(8,128)(2,1)}, bf16[1664,1024]{1,0:T(8,128)(2,1)}, u32[]{:S(2)}, u32[]{:S(2)}) collective-permute-start(bf16[1664,1024]{1,0:T(8,128)(2,1)} %bitcast.113), channel_id=1, source_target_pairs={{0,2},{2,0},{4,6},{6,4},{8,10},{10,8},{12,14},{14,12},{16,18},{18,... | collective-permute-start | bytes 10223624 | tf_op jit(solution)/shard_map/ppermute | solution.py:151
  24.0 147.0 %collective-permute-start.2 = (bf16[1024,1664]{1,0:T(8,128)(2,1)}, bf16[1024,1664]{1,0:T(8,128)(2,1)}, u32[]{:S(2)}, u32[]{:S(2)}) collective-permute-start(bf16[1024,1664]{1,0:T(8,128)(2,1)} %bitcast.117), channel_id=1, source_target_pairs={{0,2},{2,0},{4,6},{6,4},{8,10},{10,8},{12,14},{14,12},{16,18},{18,... | collective-permute-start | bytes 10223624 | tf_op jit(solution)/shard_map/ppermute | solution.py:151
  24.5 146.5 %collective-permute-start.4 = (bf16[1664,1024]{1,0:T(8,128)(2,1)}, bf16[1664,1024]{1,0:T(8,128)(2,1)}, u32[]{:S(2)}, u32[]{:S(2)}) collective-permute-start(bf16[1664,1024]{1,0:T(8,128)(2,1)} %bitcast.114), channel_id=1, source_target_pairs={{0,1},{1,0},{2,3},{3,2},{4,5},{5,4},{6,7},{7,6},{8,9},{9,8},{10,11... | collective-permute-start | bytes 10223624 | tf_op jit(solution)/shard_map/ppermute | solution.py:154
  24.5 146.5 %collective-permute-start.5 = (bf16[1024,1664]{1,0:T(8,128)(2,1)}, bf16[1024,1664]{1,0:T(8,128)(2,1)}, u32[]{:S(2)}, u32[]{:S(2)}) collective-permute-start(bf16[1024,1664]{1,0:T(8,128)(2,1)} %bitcast.118), channel_id=1, source_target_pairs={{0,1},{1,0},{2,3},{3,2},{4,5},{5,4},{6,7},{7,6},{8,9},{9,8},{10,11... | collective-permute-start | bytes 10223624 | tf_op jit(solution)/shard_map/ppermute | solution.py:154
  80.5 111.5 %copy-start.4 = (bf16[4,192,1664]{2,1,0:T(8,128)(2,1)}, bf16[4,192,1664]{2,1,0:T(8,128)(2,1)S(1)}, u32[]{:S(2)}) copy-start(bf16[4,192,1664]{2,1,0:T(8,128)(2,1)S(1)} %all-to-all-done) | copy-start | bytes 7667716
  80.5 90.5 %collective-permute-start.6 = (bf16[768,1664]{1,0:T(8,128)(2,1)S(1)}, bf16[768,1664]{1,0:T(8,128)(2,1)}, u32[]{:S(2)}, u32[]{:S(2)}) collective-permute-start(bf16[768,1664]{1,0:T(8,128)(2,1)S(1)} %bitcast.102), channel_id=1, source_target_pairs={{0,4},{2,6},{4,0},{6,2},{8,12},{10,14},{12,8},{14,10},{16,20},{18,... | collective-permute-start | bytes 7667720 | tf_op jit(solution)/shard_map/ppermute | solution.py:151
  99.5 92.6 %collective-permute-start.1 = (bf16[1664,1024]{1,0:T(8,128)(2,1)}, bf16[1664,1024]{1,0:T(8,128)(2,1)S(1)}, u32[]{:S(2)}, u32[]{:S(2)}) collective-permute-start(bf16[1664,1024]{1,0:T(8,128)(2,1)} %collective-permute-done.refs_0_), channel_id=1, source_target_pairs={{0,1},{1,0},{2,3},{3,2},{4,5},{5,4},{6,7},{7,6},{8,9},{9,8},{10,11... | collective-permute-start | bytes 10223624 | tf_op jit(solution)/shard_map/ppermute | solution.py:154
  171.0 21.1 %collective-permute-start.3 = (bf16[1024,1664]{1,0:T(8,128)(2,1)}, bf16[1024,1664]{1,0:T(8,128)(2,1)}, u32[]{:S(2)}, u32[]{:S(2)}) collective-permute-start(bf16[1024,1664]{1,0:T(8,128)(2,1)} %collective-permute-done.2.refs_2_), channel_id=1, source_target_pairs={{0,1},{1,0},{2,3},{3,2},{4,5},{5,4},{6,7},{7,6},{8,9},{9,8},{10,11... | collective-permute-start | bytes 10223624 | tf_op jit(solution)/shard_map/ppermute | solution.py:154
  192.1 1.7 copy-start.14
  215.3 58.1 %collective-permute-start.7 = (bf16[768,1664]{1,0:T(8,128)(2,1)}, bf16[768,1664]{1,0:T(8,128)(2,1)S(1)}, u32[]{:S(2)}, u32[]{:S(2)}) collective-permute-start(bf16[768,1664]{1,0:T(8,128)(2,1)} %shard_map.80), channel_id=1, source_target_pairs={{0,4},{2,6},{4,0},{6,2},{8,12},{10,14},{12,8},{14,10},{16,20},{18,... | collective-permute-start | bytes 7667720 | tf_op jit(solution)/shard_map/ppermute | solution.py:151
  277.8 62.7 %all-to-all-start.1 = ((bf16[4,192,1664]{2,1,0:T(8,128)(2,1)}), bf16[4,192,1664]{2,1,0:T(8,128)(2,1)S(1)}, u32[]{:S(2)}, u32[]{:S(2)}) async-start(bf16[4,192,1664]{2,1,0:T(8,128)(2,1)} %bitcast.7), calls=%async_computation.1 | async-start | bytes 5111808 | tf_op jit(solution)/shard_map/all_to_all | solution.py:198
  282.6 75.1 %all-gather.3.cloned.1.call-start = ((), (), s32[]{:S(2)}) async-start(), calls=%async_computation.4 | async-start | bytes 2555904 | tf_op jit(solution)/shard_map/all_gather | solution.py:217
  284.0 56.6 %copy-start.12 = (f32[256]{0:T(256)}, f32[256]{0:T(256)S(1)}, u32[]{:S(2)}) copy-start(f32[256]{0:T(256)S(1)} %get-tuple-element.13) | copy-start | bytes 3076
  284.0 56.5 %copy-start.13 = (f32[256]{0:T(256)}, f32[256]{0:T(256)S(1)}, u32[]{:S(2)}) copy-start(f32[256]{0:T(256)S(1)} %get-tuple-element.14) | copy-start | bytes 3076
  340.5 1.5 copy-start.5
  342.0 1.8 copy-start.8
  342.0 1.8 copy-start.10
  346.8 16.1 %copy-start.3 = (bf16[256,1664]{1,0:T(8,128)(2,1)}, bf16[256,1664]{1,0:T(8,128)(2,1)S(1)}, u32[]{:S(2)}) copy-start(bf16[256,1664]{1,0:T(8,128)(2,1)S(1)} %get-tuple-element.16) | copy-start | bytes 2555908
  421.1 1.4 copy-start.1
Sparse Core Ops, SparseCore 0:
  348.5 9.0 all-gather.2

commit v2 on v1

--- a/solution.py
+++ b/solution.py
@@ -25,45 +25,46 @@
     return 0.5 * value * (1.0 + jnp.tanh(inner))
 
 
-def mlp_kernel(steps, chunk, has_base, rows_ref, *refs):
-    w_in_refs, w_out_refs = refs[0:2], refs[2:4]
-    base_ref = refs[4] if has_base else None
-    out_ref, acc_ref = refs[-2], refs[-1]
+def mlp_kernel(steps, parts, has_base, *refs):
+    rows_refs, refs = refs[:parts], refs[parts:]
+    w_in_refs, w_out_refs, refs = refs[0:2], refs[2:4], refs[4:]
+    base_refs = refs[:parts] if has_base else None
+    out_refs, acc_refs = refs[-2 * parts : -parts], refs[-parts:]
     j = pl.program_id(0)
-    count = rows_ref.shape[0]
 
     @pl.when(j == 0)
     def _():
-        if has_base:
-            acc_ref[...] = base_ref[...].astype(jnp.float32)
-        else:
-            acc_ref[...] = jnp.zeros_like(acc_ref)
+        for p in range(parts):
+            if has_base:
+                acc_refs[p][...] = base_refs[p][...].astype(jnp.float32)
+            else:
+                acc_refs[p][...] = jnp.zeros_like(acc_refs[p])
 
     for block in range(2):
 
         @pl.when(j // steps == block)
         def _():
-            for start in range(0, count, chunk):
-                part = pl.ds(start, chunk)
+            for p in range(parts):
                 up = jnp.dot(
-                    rows_ref[part, :], w_in_refs[block][...], preferred_element_type=jnp.float32
+                    rows_refs[p][...], w_in_refs[block][...], preferred_element_type=jnp.float32
                 )
                 hidden = gelu(up).astype(jnp.bfloat16)
-                acc_ref[part, :] += jnp.dot(
+                acc_refs[p][...] += jnp.dot(
                     hidden, w_out_refs[block][...], preferred_element_type=jnp.float32
                 )
 
     @pl.when(j == 2 * steps - 1)
     def _():
-        out_ref[...] = acc_ref[...].astype(out_ref.dtype)
-
-
-def mlp(rows, w_ins, w_outs, base, out_dtype):
-    count, width = rows.shape
+        for p in range(parts):
+            out_refs[p][...] = acc_refs[p][...].astype(out_refs[p].dtype)
+
+
+def mlp(rows, w_ins, w_outs, base, out_dtype, most=512):
+    parts = len(rows)
+    count, width = rows[0].shape
     units = w_ins[0].shape[1]
-    tile = 512 if units % 512 == 0 else units
+    tile = most if units % most == 0 else units
     steps = units // tile
-    chunk = 256 if count % 256 == 0 else count
 
     def in_map(block):
         return lambda j: (0, jnp.clip(j - block * steps, 0, steps - 1))
@@ -72,27 +73,27 @@
         return lambda j: (jnp.clip(j - block * steps, 0, steps - 1), 0)
 
     whole = pl.BlockSpec((count, width), lambda j: (0, 0))
-    in_specs = [whole]
+    in_specs = [whole] * parts
     in_specs += [pl.BlockSpec((width, tile), in_map(b)) for b in range(2)]
     in_specs += [pl.BlockSpec((tile, width), out_map(b)) for b in range(2)]
-    operands = [rows, *w_ins, *w_outs]
+    operands = [*rows, *w_ins, *w_outs]
     if base is not None:
-        in_specs.append(whole)
-        operands.append(base)
+        in_specs += [whole] * parts
+        operands += [*base]
     return pl.pallas_call(
-        functools.partial(mlp_kernel, steps, chunk, base is not None),
+        functools.partial(mlp_kernel, steps, parts, base is not None),
         grid=(2 * steps,),
-        out_shape=jax.ShapeDtypeStruct((count, width), out_dtype),
+        out_shape=[jax.ShapeDtypeStruct((count, width), out_dtype)] * parts,
         in_specs=in_specs,
-        out_specs=whole,
-        scratch_shapes=[pltpu.VMEM((count, width), jnp.float32)],
+        out_specs=[whole] * parts,
+        scratch_shapes=[pltpu.VMEM((count, width), jnp.float32)] * parts,
         compiler_params=pltpu.CompilerParams(
-            vmem_limit_bytes=56 * MIB, dimension_semantics=("arbitrary",)
+            vmem_limit_bytes=60 * MIB, dimension_semantics=("arbitrary",)
         ),
         cost_estimate=pl.CostEstimate(
-            flops=8 * count * width * units,
-            bytes_accessed=8 * width * units + 10 * count * width,
-            transcendentals=2 * count * units,
+            flops=8 * parts * count * width * units,
+            bytes_accessed=8 * width * units + 10 * parts * count * width,
+            transcendentals=2 * parts * count * units,
         ),
     )(*operands)
 
@@ -154,9 +155,8 @@
         return lax.ppermute(value, "seq", [(0, 1), (1, 0)])
 
     own_weights = (w_in[0], w_out[0])
+    far_weights = tuple(across(w, 1) for w in own_weights)
     core_weights = tuple(other_core(w) for w in own_weights)
-    far_weights = tuple(across(w, 1) for w in own_weights)
-    far_core_weights = tuple(other_core(w) for w in far_weights)
 
     own_tokens = tokens[0]
     own_ids = expert_ids[0]
@@ -173,51 +173,71 @@
     position = jnp.sum(before * onehot, axis=1)
     slot_index = jnp.where(position < slots, pair_ids * slots + position, -1)
     slot_index = slot_index.reshape(row_count, 2)
-    slot_range = jnp.arange(experts * slots, dtype=jnp.int32)
-    is_first = slot_index[:, 0:1] == slot_range[None, :]
-    is_second = slot_index[:, 1:2] == slot_range[None, :]
-    select = (is_first | is_second).astype(jnp.bfloat16)
-    packed = lax.dot_general(
-        select, normed, (((0,), (0,)), ((), ())), preferred_element_type=jnp.float32
-    ).astype(jnp.bfloat16)
-    outgoing = packed.reshape(experts, slots, width)
-    received = lax.all_to_all(
-        outgoing, "expert", split_axis=0, concat_axis=0, tiled=True, axis_index_groups=columns
-    )
-    near_rows = received.reshape(experts * slots, width)
-    far_rows = across(near_rows, 2)
+    parts = 2 if slots % 2 == 0 else 1
+    part_slots = slots // parts
+    slot_range = (
+        jnp.arange(experts, dtype=jnp.int32)[:, None] * slots
+        + jnp.arange(part_slots, dtype=jnp.int32)[None, :]
+    ).reshape(1, experts * part_slots)
+
+    def between_planes(value):
+        return lax.all_to_all(
+            value.reshape(experts, part_slots, width),
+            "expert",
+            split_axis=0,
+            concat_axis=0,
+            tiled=True,
+            axis_index_groups=columns,
+        ).reshape(experts * part_slots, width)
+
+    near_rows, far_rows, gate_parts = [], [], []
+    for p in range(parts):
+        is_first = slot_index[:, 0:1] == slot_range + p * part_slots
+        is_second = slot_index[:, 1:2] == slot_range + p * part_slots
+        select = (is_first | is_second).astype(jnp.bfloat16)
+        packed = lax.dot_general(
+            select, normed, (((0,), (0,)), ((), ())), preferred_element_type=jnp.float32
+        ).astype(jnp.bfloat16)
+        near_rows.append(between_planes(packed))
+        far_rows.append(across(near_rows[p], 2))
+        gates = jnp.where(is_first, first_gate[:, None], 0.0) + jnp.where(
+            is_second, second_gate[:, None], 0.0
+        )
+        high = gates.astype(jnp.bfloat16)
+        gate_parts.append((high, (gates - high.astype(jnp.float32)).astype(jnp.bfloat16)))
 
     chip_in, chip_out = zip(own_weights, core_weights)
-    next_in, next_out = zip(far_weights, far_core_weights)
     near_sum = mlp(near_rows, chip_in, chip_out, None, jnp.float32)
     far_sum = mlp(far_rows, chip_in, chip_out, None, jnp.float32)
-    far_sum = mlp(far_rows, next_in, next_out, far_sum, jnp.bfloat16)
-    arrived = across(far_sum, 2)
+    far_weights, near_sum, far_sum = lax.optimization_barrier((far_weights, near_sum, far_sum))
+    far_core_weights = tuple(other_core(w) for w in far_weights)
+    next_in, next_out = zip(far_weights, far_core_weights)
+    sent = []
+    for p in range(parts):
+        sent += mlp(far_rows[p : p + 1], next_in, next_out, far_sum[p : p + 1], jnp.bfloat16)
+        if p + 1 < parts:
+            sent[p], far_sum = lax.optimization_barrier((sent[p], far_sum))
+    arrived = [across(value, 2) for value in sent]
     near_sum = mlp(near_rows, next_in, next_out, near_sum, jnp.float32)
-    summed = (near_sum + arrived.astype(jnp.float32)).astype(jnp.bfloat16)
-    merged = lax.all_to_all(
-        summed.reshape(experts, slots, width),
-        "expert",
-        split_axis=0,
-        concat_axis=0,
-        tiled=True,
-        axis_index_groups=columns,
-    ).reshape(experts * slots, width)
-
-    gates = jnp.where(is_first, first_gate[:, None], 0.0) + jnp.where(
-        is_second, second_gate[:, None], 0.0
-    )
-    high = gates.astype(jnp.bfloat16)
-    low = (gates - high.astype(jnp.float32)).astype(jnp.bfloat16)
-    combined = jnp.dot(high, merged, preferred_element_type=jnp.float32) + jnp.dot(
-        low, merged, preferred_element_type=jnp.float32
-    )
-    mixed = (own_tokens.astype(jnp.float32) + combined).astype(jnp.bfloat16)
+    combined = own_tokens.astype(jnp.float32)
+    for p in range(parts):
+        summed = (near_sum[p] + arrived[p].astype(jnp.float32)).astype(jnp.bfloat16)
+        merged = between_planes(summed)
+        for gate in gate_parts[p]:
+            combined += jnp.dot(gate, merged, preferred_element_type=jnp.float32)
+    mixed = combined.astype(jnp.bfloat16)
     attn_local = layer_norm(mixed)
-    attn_in = lax.all_gather(attn_local[None], "seq", axis=0, tiled=True)
-    images = attn_in.shape[0]
-    proj = jnp.einsum("cdf,ird->cifr", w_qkv, attn_in, preferred_element_type=jnp.float32).astype(
-        jnp.bfloat16
+    attn_other = other_core(attn_local)
+    own_proj, other_proj = [
+        jnp.einsum("cdf,rd->cfr", w_qkv, value, preferred_element_type=jnp.float32).astype(
+            jnp.bfloat16
+        )
+        for value in (attn_local, attn_other)
+    ]
+    images = 2
+    is_low = lax.axis_index("seq") == 0
+    proj = jnp.stack(
+        [jnp.where(is_low, own_proj, other_proj), jnp.where(is_low, other_proj, own_proj)], axis=1
     )
     heads = proj.shape[2] // HD
     pairs = images * heads

time: 459 us -> 434 us (0.946)
  waiting for transfers between devices: 223 us -> 200 us
  between operations: 14.4 us -> 1.05 us
  starting transfers between devices: 16.7 us -> 28.6 us
    all_to_all x2 -> x4, waiting for transfers between devices: 112 us -> 79.1 us  [between_planes(): lax.all_to_all(value.reshape(experts, part_slots, width), 'expert', split...]
    ppermute x4 -> x5, waiting for transfers between devices: 0.01 us -> 10.7 us  [other_core(): return lax.ppermute(value, 'seq', [(0, 1), (1, 0)])]
    all_gather x1 -> x0, waiting for transfers between devices: 9.26 us -> none  [shards(): attn_in = lax.all_gather(attn_local[None], 'seq', axis=0, tiled=True)]
    ppermute x4 -> x6, waiting for transfers between devices: 102 us -> 110 us  [across(): return lax.ppermute(value, 'expert', [(p, p ^ bit) for p in range(places)])]
    all_to_all x2 -> x4, starting transfers between devices: 11.1 us -> 19.4 us  [between_planes(): lax.all_to_all(value.reshape(experts, part_slots, width), 'expert', split...]
    pallas_call x4 -> x5, Pallas kernels: 86.1 us -> 88.4 us  [mlp(): pl.pallas_call(functools.partial(mlp_kernel, steps, parts, base is not No...]
    dot_general x3 -> x6, matrix products: 10 us -> 10.8 us  [the longest x4 5.78 us: shards(): combined += jnp.dot(gate, merged, preferred_element_type=jnp.float32)]
  transfers between devices with their start and end apart: 11 -> 15, of which waited for: 6 -> 9; matrix products, arithmetic and copies ran while one was open for 0% -> 3% of each run, Pallas kernels for 14% -> 17%
where the time goes in v2:
time: 434 us
  waiting for transfers between devices  200 us (46%)
  Pallas kernels  99 us (23%)
  blocking collectives  71.5 us (16%)
  starting transfers between devices  28.6 us (7%)
  matrix products  15.6 us (4%)
  other arithmetic  9.17 us (2%)
  local copies, waits for them, and re-layouts  8.47 us (2%)
    ppermute x6, waiting for transfers between devices, across(): return lax.ppermute(value, 'expert', [(p, p ^ bit) for p in range(places)])  110 us
    pallas_call x5, Pallas kernels, mlp(): pl.pallas_call(functools.partial(mlp_kernel, steps, parts, base is not No...  88.4 us
    all_to_all x4, waiting for transfers between devices, between_planes(): lax.all_to_all(value.reshape(experts, part_slots, width), 'expert', split...  79.1 us
    all_to_all x1, blocking collectives, shards(): lax.all_to_all(leaving, 'expert', split_axis=0, concat_axis=0, tiled=True)  55.7 us
    all_to_all x4, starting transfers between devices, between_planes(): lax.all_to_all(value.reshape(experts, part_slots, width), 'expert', split...  19.4 us
    all_to_all x1, blocking collectives, shards(): lax.all_to_all(result, 'expert', split_axis=0, concat_axis=0, tiled=True)  15.8 us
    ppermute x5, waiting for transfers between devices, other_core(): return lax.ppermute(value, 'seq', [(0, 1), (1, 0)])  10.7 us
    pallas_call x1, Pallas kernels, attention(): pl.pallas_call(functools.partial(attention_kernel, key_tile), grid=(colum...  10.6 us
  transfers between devices with their start and end apart: 15, of which 9 were waited for; matrix products, arithmetic and copies ran while one was open for 3% of the time, Pallas kernels for 17%

profile of v2, /device:TPU:0, one launch (start us, length us, event | category | flops | bytes accessed | tf_op | source)
XLA Modules:
  0.0 433.6 jit_solution(8639051795345500358)
XLA Ops:
  0.7 0.9 copy.29
  1.9 1.2 reduce-window.6
  4.8 1.8 convolution_convert_fusion
  6.6 6.3 %all-to-all-start.1 = ((bf16[4,96,1664]{2,1,0:T(8,128)(2,1)}), bf16[4,96,1664]{2,1,0:T(8,128)(2,1)S(1)}, u32[]{:S(2)}, u32[]{:S(2)}) async-start(bf16[4,96,1664]{2,1,0:T(8,128)(2,1)} %bitcast.5), calls=%async_computation.1 | async-start | bytes 2555904 | tf_op jit(solution)/shard_map/all_to_all | solution.py:184
  12.9 0.5 collective-permute-start.3
  13.5 1.8 convolution_convert_fusion.1
  15.3 28.3 %all-to-all-done.1 = bf16[4,96,1664]{2,1,0:T(8,128)(2,1)S(1)} async-done(((bf16[4,96,1664]{2,1,0:T(8,128)(2,1)}), bf16[4,96,1664]{2,1,0:T(8,128)(2,1)S(1)}, u32[]{:S(2)}, u32[]{:S(2)}) %all-to-all-start.1) | async-done | bytes 1277984 | tf_op jit(solution)/shard_map/all_to_all | solution.py:184
  43.6 3.7 all-to-all-start
  47.3 1.6 collective-permute-start
  48.8 0.5 collective-permute-start.1
  49.4 1.5 collective-permute-start.5
  50.9 26.3 %all-to-all-done = bf16[4,96,1664]{2,1,0:T(8,128)(2,1)S(1)} async-done(((bf16[4,96,1664]{2,1,0:T(8,128)(2,1)}), bf16[4,96,1664]{2,1,0:T(8,128)(2,1)S(1)}, u32[]{:S(2)}, u32[]{:S(2)}) %all-to-all-start) | async-done | bytes 1277984 | tf_op jit(solution)/shard_map/all_to_all | solution.py:184
  77.2 1.5 collective-permute-start.4
  78.8 20.4 %shard_map.77 = (f32[384,1664]{1,0:T(8,128)}, f32[384,1664]{1,0:T(8,128)}) custom-call(bf16[384,1664]{1,0:T(8,128)(2,1)} %bitcast.125, bf16[384,1664]{1,0:T(8,128)(2,1)} %bitcast.122, bf16[1664,1024]{1,0:T(8,128)(2,1)} %bitcast.131, bf16[1664,1024]{1,0:T(8,128)(2,1)} %collective-permute-done.2.refs_3_, bf16[1024,1664]{1,0:T(8,128)(2,1)} %bitcast.135, ...), custom_call_target="tpu_custom_call" | custom-call | flops 10468982784 | bytes 26411008 | tf_op jit(solution)/shard_map/pallas_call | solution.py:83
  99.2 7.2 %collective-permute-done.4.refs_0_ = bf16[384,1664]{1,0:T(8,128)(2,1)} collective-permute-done((bf16[384,1664]{1,0:T(8,128)(2,1)S(1)}, bf16[384,1664]{1,0:T(8,128)(2,1)}, u32[]{:S(2)}, u32[]{:S(2)}) %collective-permute-start.4) | collective-permute-done | bytes 1277984 | tf_op jit(solution)/shard_map/ppermute | solution.py:152
  106.4 20.4 %shard_map.78 = (f32[384,1664]{1,0:T(8,128)}, f32[384,1664]{1,0:T(8,128)}) custom-call(bf16[384,1664]{1,0:T(8,128)(2,1)} %collective-permute-done.4.refs_0_, bf16[384,1664]{1,0:T(8,128)(2,1)} %collective-permute-done.5.refs_1_.refs_0_, bf16[1664,1024]{1,0:T(8,128)(2,1)} %bitcast.132, bf16[1664,1024]{1,0:T(8,128)(2,1)} %collective-permute-done.2.refs_3_, ...), custom_call_target="tpu_custom_call" | custom-call | flops 10468982784 | bytes 26411008 | tf_op jit(solution)/shard_map/pallas_call | solution.py:83
  126.8 68.6 %collective-permute-done.1.refs_4_.refs_3_ = bf16[1024,1664]{1,0:T(8,128)(2,1)} collective-permute-done((bf16[1024,1664]{1,0:T(8,128)(2,1)}, bf16[1024,1664]{1,0:T(8,128)(2,1)}, u32[]{:S(2)}, u32[]{:S(2)}) %collective-permute-start.1) | collective-permute-done | bytes 3407904 | tf_op jit(solution)/shard_map/ppermute | solution.py:152
  195.4 0.5 collective-permute-start.7
  195.9 5.9 %collective-permute-done.6.refs_3_.refs_2_ = bf16[1664,1024]{1,0:T(8,128)(2,1)} collective-permute-done((bf16[1664,1024]{1,0:T(8,128)(2,1)}, bf16[1664,1024]{1,0:T(8,128)(2,1)}, u32[]{:S(2)}, u32[]{:S(2)}) %collective-permute-start.6) | collective-permute-done | bytes 3407904 | tf_op jit(solution)/shard_map/ppermute | solution.py:155
  201.8 4.9 %collective-permute-done.7.refs_5_.refs_4_ = bf16[1024,1664]{1,0:T(8,128)(2,1)} collective-permute-done((bf16[1024,1664]{1,0:T(8,128)(2,1)}, bf16[1024,1664]{1,0:T(8,128)(2,1)}, u32[]{:S(2)}, u32[]{:S(2)}) %collective-permute-start.7) | collective-permute-done | bytes 3407904 | tf_op jit(solution)/shard_map/ppermute | solution.py:155
  206.6 12.8 %shard_map.80 = bf16[384,1664]{1,0:T(8,128)(2,1)} custom-call(bf16[384,1664]{1,0:T(8,128)(2,1)} %collective-permute-done.4.refs_0_, bf16[1664,1024]{1,0:T(8,128)(2,1)} %collective-permute-done.refs_2_.refs_1_, bf16[1664,1024]{1,0:T(8,128)(2,1)} %collective-permute-done.6.refs_3_.refs_2_, bf16[1024,1664]{1,0:T(8,128)(2,1)} %collective-permute-done.1.refs_4_.refs_3_, ...), custom_call_target="tpu_custom_call" | custom-call | flops 5234491392 | bytes 20021248 | tf_op jit(solution)/shard_map/pallas_call | solution.py:83
  219.5 1.5 collective-permute-start.8
  221.0 21.9 %shard_map.79 = (f32[384,1664]{1,0:T(8,128)}, f32[384,1664]{1,0:T(8,128)}) custom-call(bf16[384,1664]{1,0:T(8,128)(2,1)} %bitcast.126, bf16[384,1664]{1,0:T(8,128)(2,1)} %bitcast.123, bf16[1664,1024]{1,0:T(8,128)(2,1)} %collective-permute-done.refs_2_.refs_1_, bf16[1664,1024]{1,0:T(8,128)(2,1)} %collective-permute-done.6.refs_3_.refs_2_, ...), custom_call_target="tpu_custom_call" | custom-call | flops 10468982784 | bytes 26411008 | tf_op jit(solution)/shard_map/pallas_call | solution.py:83
  242.9 6.9 %collective-permute-done.8 = bf16[384,1664]{1,0:T(8,128)(2,1)S(1)} collective-permute-done((bf16[384,1664]{1,0:T(8,128)(2,1)}, bf16[384,1664]{1,0:T(8,128)(2,1)S(1)}, u32[]{:S(2)}, u32[]{:S(2)}) %collective-permute-start.8) | collective-permute-done | bytes 1277984 | tf_op jit(solution)/shard_map/ppermute | solution.py:152
  249.8 3.0 add_convert_fusion.1
  252.8 4.5 %all-to-all-start.2 = ((bf16[4,96,1664]{2,1,0:T(8,128)(2,1)}), bf16[4,96,1664]{2,1,0:T(8,128)(2,1)S(1)}, u32[]{:S(2)}, u32[]{:S(2)}) async-start(bf16[4,96,1664]{2,1,0:T(8,128)(2,1)} %bitcast.9), calls=%async_computation.2 | async-start | bytes 2555904 | tf_op jit(solution)/shard_map/all_to_all | solution.py:184
  257.3 12.8 %shard_map.81 = bf16[384,1664]{1,0:T(8,128)(2,1)} custom-call(bf16[384,1664]{1,0:T(8,128)(2,1)} %collective-permute-done.5.refs_1_.refs_0_, bf16[1664,1024]{1,0:T(8,128)(2,1)} %collective-permute-done.refs_2_.refs_1_, bf16[1664,1024]{1,0:T(8,128)(2,1)} %collective-permute-done.6.refs_3_.refs_2_, bf16[1024,1664]{1,0:T(8,128)(2,1)} %collective-permute-done.1.refs_4_.refs_3_, ...), custom_call_target="tpu_custom_call" | custom-call | flops 5234491392 | bytes 20021248 | tf_op jit(solution)/shard_map/pallas_call | solution.py:83
  270.2 1.5 collective-permute-start.9
  271.7 27.7 %collective-permute-done.9 = bf16[384,1664]{1,0:T(8,128)(2,1)S(1)} collective-permute-done((bf16[384,1664]{1,0:T(8,128)(2,1)}, bf16[384,1664]{1,0:T(8,128)(2,1)S(1)}, u32[]{:S(2)}, u32[]{:S(2)}) %collective-permute-start.9) | collective-permute-done | bytes 1277984 | tf_op jit(solution)/shard_map/ppermute | solution.py:152
  299.4 3.0 add_convert_fusion
  302.4 4.8 %all-to-all-start.3 = ((bf16[4,96,1664]{2,1,0:T(8,128)(2,1)}), bf16[4,96,1664]{2,1,0:T(8,128)(2,1)S(1)}, u32[]{:S(2)}, u32[]{:S(2)}) async-start(bf16[4,96,1664]{2,1,0:T(8,128)(2,1)} %bitcast.115), calls=%async_computation.3 | async-start | bytes 2555904 | tf_op jit(solution)/shard_map/all_to_all | solution.py:184
  307.4 1.1 select_reduce_fusion.1
  308.6 0.7 convolution_add_fusion.3
  309.4 2.0 convolution_add_fusion.2
  311.3 24.5 %all-to-all-done.3 = bf16[4,96,1664]{2,1,0:T(8,128)(2,1)S(1)} async-done(((bf16[4,96,1664]{2,1,0:T(8,128)(2,1)}), bf16[4,96,1664]{2,1,0:T(8,128)(2,1)S(1)}, u32[]{:S(2)}, u32[]{:S(2)}) %all-to-all-start.3) | async-done | bytes 1277984 | tf_op jit(solution)/shard_map/all_to_all | solution.py:184
  335.8 2.2 convolution_add_fusion.1
  338.0 0.9 convert_reduce_fusion
  338.9 0.4 fusion.6
  339.3 0.5 copy-done.1
  340.2 3.7 convolution_convert_fusion.3
  343.9 1.4 select_bitcast_fusion.1
  345.9 55.7 %all_to_all.30 = bf16[16,104,640]{2,1,0:T(8,128)(2,1)S(1)} all-to-all(bf16[16,104,640]{2,1,0:T(8,128)(2,1)S(1)} %bitcast.113), channel_id=1, replica_groups=mesh['group'=1,'expert'=16,'seq'=2] {'expert'}, dimensions={0} | all-to-all | bytes 4259840 | tf_op jit(solution)/shard_map/all_to_all | solution.py:253
  401.6 1.3 slice_bitcast_fusion
  402.9 1.6 copy.34
  404.5 1.2 copy.40
  405.8 10.6 %shard_map.82 = bf16[104,2048]{1,0:T(8,128)(2,1)S(1)} custom-call(bf16[104,2048]{1,0:T(8,128)(2,1)S(1)} %copy_bitcast_fusion.q_ref, bf16[4096,104]{1,0:T(8,128)(2,1)S(1)} %bitcast.107, bf16[104,4096]{1,0:T(8,128)(2,1)S(1)} %bitcast.108), custom_call_target="tpu_custom_call" | custom-call | flops 3489660928 | bytes 2555904 | tf_op jit(solution)/shard_map/pallas_call | solution.py:123
  416.5 15.8 %all_to_all.31 = bf16[16,104,128]{2,1,0:T(8,128)(2,1)S(1)} all-to-all(bf16[16,104,128]{2,1,0:T(8,128)(2,1)S(1)} %bitcast_bitcast_fusion), channel_id=1, replica_groups=mesh['group'=1,'expert'=16,'seq'=2] {'expert'}, dimensions={0} | all-to-all | bytes 851968 | tf_op jit(solution)/shard_map/all_to_all | solution.py:260
  432.6 1.0 reshape.167
  (76 shorter events, 3.6 us)
Async XLA Ops:
  0.6 306.8 %copy-start = (bf16[1664,4]{0,1:T(4,128)(2,1)S(1)}, bf16[1664,4]{0,1:T(4,128)(2,1)}, u32[]{:S(2)}) copy-start(bf16[1664,4]{0,1:T(4,128)(2,1)} %param.7) | copy-start | bytes 39940
  0.6 3.5 copy-start.2
  4.0 9.5 %copy-start.7 = (s32[256]{0:T(256)}, s32[256]{0:T(256)S(1)}, u32[]{:S(2)}) copy-start(s32[256]{0:T(256)S(1)} %get-tuple-element.32) | copy-start | bytes 3076
  4.0 9.5 %copy-start.10 = (s32[256]{0:T(256)}, s32[256]{0:T(256)S(1)}, u32[]{:S(2)}) copy-start(s32[256]{0:T(256)S(1)} %get-tuple-element.33) | copy-start | bytes 3076
  4.1 9.3 %copy-start.5 = (s32[384]{0:T(512)}, s32[384]{0:T(512)S(1)}, u32[]{:S(2)}) copy-start(s32[384]{0:T(512)S(1)} %add.121) | copy-start | bytes 4612
  4.2 2.4 copy-start.13
  4.4 9.1 %copy-start.15 = (f32[256]{0:T(256)}, f32[256]{0:T(256)S(1)}, u32[]{:S(2)}) copy-start(f32[256]{0:T(256)S(1)} %broadcast_multiply_fusion.1) | copy-start | bytes 3076
  4.8 8.7 %copy-start.16 = (f32[256]{0:T(256)}, f32[256]{0:T(256)S(1)}, u32[]{:S(2)}) copy-start(f32[256]{0:T(256)S(1)} %add_rsqrt_fusion.1) | copy-start | bytes 3076
  6.6 37.0 %all-to-all-start.1 = ((bf16[4,96,1664]{2,1,0:T(8,128)(2,1)}), bf16[4,96,1664]{2,1,0:T(8,128)(2,1)S(1)}, u32[]{:S(2)}, u32[]{:S(2)}) async-start(bf16[4,96,1664]{2,1,0:T(8,128)(2,1)} %bitcast.5), calls=%async_computation.1 | async-start | bytes 2555904 | tf_op jit(solution)/shard_map/all_to_all | solution.py:184
  12.9 64.3 %collective-permute-start.2 = (bf16[1664,1024]{1,0:T(8,128)(2,1)}, bf16[1664,1024]{1,0:T(8,128)(2,1)}, u32[]{:S(2)}, u32[]{:S(2)}) collective-permute-start(bf16[1664,1024]{1,0:T(8,128)(2,1)} %bitcast.129), channel_id=1, source_target_pairs={{0,1},{1,0},{2,3},{3,2},{4,5},{5,4},{6,7},{7,6},{8,9},{9,8},{10,11... | collective-permute-start | bytes 10223624 | tf_op jit(solution)/shard_map/ppermute | solution.py:155
  12.9 65.8 %collective-permute-start.3 = (bf16[1024,1664]{1,0:T(8,128)(2,1)}, bf16[1024,1664]{1,0:T(8,128)(2,1)}, u32[]{:S(2)}, u32[]{:S(2)}) collective-permute-start(bf16[1024,1664]{1,0:T(8,128)(2,1)} %bitcast.133), channel_id=1, source_target_pairs={{0,1},{1,0},{2,3},{3,2},{4,5},{5,4},{6,7},{7,6},{8,9},{9,8},{10,11... | collective-permute-start | bytes 10223624 | tf_op jit(solution)/shard_map/ppermute | solution.py:155
  43.6 35.2 %copy-start.3 = (bf16[4,96,1664]{2,1,0:T(8,128)(2,1)}, bf16[4,96,1664]{2,1,0:T(8,128)(2,1)S(1)}, u32[]{:S(2)}) copy-start(bf16[4,96,1664]{2,1,0:T(8,128)(2,1)S(1)} %all-to-all-done.1) | copy-start | bytes 3833860
  43.6 33.7 %all-to-all-start = ((bf16[4,96,1664]{2,1,0:T(8,128)(2,1)}), bf16[4,96,1664]{2,1,0:T(8,128)(2,1)S(1)}, u32[]{:S(2)}, u32[]{:S(2)}) async-start(bf16[4,96,1664]{2,1,0:T(8,128)(2,1)} %bitcast.127), calls=%async_computation | async-start | bytes 2555904 | tf_op jit(solution)/shard_map/all_to_all | solution.py:184
  47.3 79.5 %collective-permute-start = (bf16[1664,1024]{1,0:T(8,128)(2,1)}, bf16[1664,1024]{1,0:T(8,128)(2,1)}, u32[]{:S(2)}, u32[]{:S(2)}) collective-permute-start(bf16[1664,1024]{1,0:T(8,128)(2,1)} %bitcast.130), channel_id=1, source_target_pairs={{0,2},{2,0},{4,6},{6,4},{8,10},{10,8},{12,14},{14,12},{16,18},{18,... | collective-permute-start | bytes 10223624 | tf_op jit(solution)/shard_map/ppermute | solution.py:152
  48.8 146.5 %collective-permute-start.1 = (bf16[1024,1664]{1,0:T(8,128)(2,1)}, bf16[1024,1664]{1,0:T(8,128)(2,1)}, u32[]{:S(2)}, u32[]{:S(2)}) collective-permute-start(bf16[1024,1664]{1,0:T(8,128)(2,1)} %bitcast.134), channel_id=1, source_target_pairs={{0,2},{2,0},{4,6},{6,4},{8,10},{10,8},{12,14},{14,12},{16,18},{18,... | collective-permute-start | bytes 10223624 | tf_op jit(solution)/shard_map/ppermute | solution.py:152
  49.4 49.8 %collective-permute-start.5 = (bf16[384,1664]{1,0:T(8,128)(2,1)S(1)}, bf16[384,1664]{1,0:T(8,128)(2,1)}, u32[]{:S(2)}, u32[]{:S(2)}) collective-permute-start(bf16[384,1664]{1,0:T(8,128)(2,1)S(1)} %bitcast.121), channel_id=1, source_target_pairs={{0,4},{2,6},{4,0},{6,2},{8,12},{10,14},{12,8},{14,10},{16,20},{18,... | collective-permute-start | bytes 3833864 | tf_op jit(solution)/shard_map/ppermute | solution.py:152
  77.2 1.5 copy-start.4
  77.2 29.1 %collective-permute-start.4 = (bf16[384,1664]{1,0:T(8,128)(2,1)S(1)}, bf16[384,1664]{1,0:T(8,128)(2,1)}, u32[]{:S(2)}, u32[]{:S(2)}) collective-permute-start(bf16[384,1664]{1,0:T(8,128)(2,1)S(1)} %bitcast.124), channel_id=1, source_target_pairs={{0,4},{2,6},{4,0},{6,2},{8,12},{10,14},{12,8},{14,10},{16,20},{18,... | collective-permute-start | bytes 3833864 | tf_op jit(solution)/shard_map/ppermute | solution.py:152
  195.4 6.4 %collective-permute-start.6 = (bf16[1664,1024]{1,0:T(8,128)(2,1)}, bf16[1664,1024]{1,0:T(8,128)(2,1)}, u32[]{:S(2)}, u32[]{:S(2)}) collective-permute-start(bf16[1664,1024]{1,0:T(8,128)(2,1)} %collective-permute-done.refs_2_.refs_1_), channel_id=1, source_target_pairs={{0,1},{1,0},{2,3},{3,2},{4,5},{5,4},{6,7},{7,6},{8,9},{9,8},{10,11... | collective-permute-start | bytes 10223624 | tf_op jit(solution)/shard_map/ppermute | solution.py:155
  195.4 11.2 %collective-permute-start.7 = (bf16[1024,1664]{1,0:T(8,128)(2,1)}, bf16[1024,1664]{1,0:T(8,128)(2,1)}, u32[]{:S(2)}, u32[]{:S(2)}) collective-permute-start(bf16[1024,1664]{1,0:T(8,128)(2,1)} %collective-permute-done.1.refs_4_.refs_3_), channel_id=1, source_target_pairs={{0,1},{1,0},{2,3},{3,2},{4,5},{5,4},{6,7},{7,6},{8,9},{9,8},{10,11... | collective-permute-start | bytes 10223624 | tf_op jit(solution)/shard_map/ppermute | solution.py:155
  219.5 30.3 %collective-permute-start.8 = (bf16[384,1664]{1,0:T(8,128)(2,1)}, bf16[384,1664]{1,0:T(8,128)(2,1)S(1)}, u32[]{:S(2)}, u32[]{:S(2)}) collective-permute-start(bf16[384,1664]{1,0:T(8,128)(2,1)} %shard_map.80), channel_id=1, source_target_pairs={{0,4},{2,6},{4,0},{6,2},{8,12},{10,14},{12,8},{14,10},{16,20},{18,... | collective-permute-start | bytes 3833864 | tf_op jit(solution)/shard_map/ppermute | solution.py:152
  252.8 49.6 %all-to-all-start.2 = ((bf16[4,96,1664]{2,1,0:T(8,128)(2,1)}), bf16[4,96,1664]{2,1,0:T(8,128)(2,1)S(1)}, u32[]{:S(2)}, u32[]{:S(2)}) async-start(bf16[4,96,1664]{2,1,0:T(8,128)(2,1)} %bitcast.9), calls=%async_computation.2 | async-start | bytes 2555904 | tf_op jit(solution)/shard_map/all_to_all | solution.py:184
  270.2 29.2 %collective-permute-start.9 = (bf16[384,1664]{1,0:T(8,128)(2,1)}, bf16[384,1664]{1,0:T(8,128)(2,1)S(1)}, u32[]{:S(2)}, u32[]{:S(2)}) collective-permute-start(bf16[384,1664]{1,0:T(8,128)(2,1)} %shard_map.81), channel_id=1, source_target_pairs={{0,4},{2,6},{4,0},{6,2},{8,12},{10,14},{12,8},{14,10},{16,20},{18,... | collective-permute-start | bytes 3833864 | tf_op jit(solution)/shard_map/ppermute | solution.py:152
  302.4 33.4 %all-to-all-start.3 = ((bf16[4,96,1664]{2,1,0:T(8,128)(2,1)}), bf16[4,96,1664]{2,1,0:T(8,128)(2,1)S(1)}, u32[]{:S(2)}, u32[]{:S(2)}) async-start(bf16[4,96,1664]{2,1,0:T(8,128)(2,1)} %bitcast.115), calls=%async_computation.3 | async-start | bytes 2555904 | tf_op jit(solution)/shard_map/all_to_all | solution.py:184
  307.2 1.4 copy-start.6
  307.2 1.4 copy-start.8
  307.2 1.4 copy-start.11
  309.3 26.5 %copy-start.9 = (s32[256]{0:T(256)S(1)}, s32[256]{0:T(256)}, u32[]{:S(2)}) copy-start(s32[256]{0:T(256)} %copy-done.7) | copy-start | bytes 3076
  309.3 26.5 %copy-start.12 = (s32[256]{0:T(256)S(1)}, s32[256]{0:T(256)}, u32[]{:S(2)}) copy-start(s32[256]{0:T(256)} %copy-done.10) | copy-start | bytes 3076
  309.3 26.5 %copy-start.14 = (s32[384]{0:T(512)S(1)}, s32[384]{0:T(512)}, u32[]{:S(2)}) copy-start(s32[384]{0:T(512)} %copy-done.13) | copy-start | bytes 4612
  338.9 0.9 copy-start.1
  340.1 3.8 collective-permute-start.10
  340.2 3.7 copy-start.17

commit v3 on v2

--- a/solution.py
+++ b/solution.py
@@ -182,35 +182,43 @@
 
     def between_planes(value):
         return lax.all_to_all(
-            value.reshape(experts, part_slots, width),
+            value.reshape(experts, -1, width),
             "expert",
             split_axis=0,
             concat_axis=0,
             tiled=True,
             axis_index_groups=columns,
-        ).reshape(experts * part_slots, width)
-
-    near_rows, far_rows, gate_parts = [], [], []
+        )
+
+    packed, gate_parts = [], []
     for p in range(parts):
         is_first = slot_index[:, 0:1] == slot_range + p * part_slots
         is_second = slot_index[:, 1:2] == slot_range + p * part_slots
         select = (is_first | is_second).astype(jnp.bfloat16)
-        packed = lax.dot_general(
+        rows = lax.dot_general(
             select, normed, (((0,), (0,)), ((), ())), preferred_element_type=jnp.float32
         ).astype(jnp.bfloat16)
-        near_rows.append(between_planes(packed))
-        far_rows.append(across(near_rows[p], 2))
+        packed.append(rows.reshape(experts, part_slots, width))
         gates = jnp.where(is_first, first_gate[:, None], 0.0) + jnp.where(
             is_second, second_gate[:, None], 0.0
         )
         high = gates.astype(jnp.bfloat16)
         gate_parts.append((high, (gates - high.astype(jnp.float32)).astype(jnp.bfloat16)))
 
+    received = between_planes(jnp.concatenate(packed, axis=1))
+    near_rows = [
+        received[:, p * part_slots : (p + 1) * part_slots].reshape(experts * part_slots, width)
+        for p in range(parts)
+    ]
+    far_rows = [across(value, 2) for value in near_rows]
     chip_in, chip_out = zip(own_weights, core_weights)
     near_sum = mlp(near_rows, chip_in, chip_out, None, jnp.float32)
     far_sum = mlp(far_rows, chip_in, chip_out, None, jnp.float32)
-    far_weights, near_sum, far_sum = lax.optimization_barrier((far_weights, near_sum, far_sum))
-    far_core_weights = tuple(other_core(w) for w in far_weights)
+    far_in, near_sum, far_sum = lax.optimization_barrier((far_weights[0], near_sum, far_sum))
+    far_core_in = other_core(far_in)
+    far_out, far_sum = lax.optimization_barrier((far_weights[1], far_sum))
+    far_weights = (far_in, far_out)
+    far_core_weights = (far_core_in, other_core(far_out))
     next_in, next_out = zip(far_weights, far_core_weights)
     sent = []
     for p in range(parts):
@@ -218,11 +226,15 @@
         if p + 1 < parts:
             sent[p], far_sum = lax.optimization_barrier((sent[p], far_sum))
     arrived = [across(value, 2) for value in sent]
-    near_sum = mlp(near_rows, next_in, next_out, near_sum, jnp.float32)
+    near_sum, sent[-1] = lax.optimization_barrier((near_sum, sent[-1]))
+    near_sum = [
+        mlp(near_rows[p : p + 1], next_in, next_out, near_sum[p : p + 1], jnp.float32)[0]
+        for p in range(parts)
+    ]
     combined = own_tokens.astype(jnp.float32)
     for p in range(parts):
         summed = (near_sum[p] + arrived[p].astype(jnp.float32)).astype(jnp.bfloat16)
-        merged = between_planes(summed)
+        merged = between_planes(summed).reshape(experts * part_slots, width)
         for gate in gate_parts[p]:
             combined += jnp.dot(gate, merged, preferred_element_type=jnp.float32)
     mixed = combined.astype(jnp.bfloat16)

time: 434 us -> 396 us (0.912)
  waiting for transfers between devices: 200 us -> 153 us
  Pallas kernels: 99 us -> 104 us
    ppermute x6, waiting for transfers between devices: 110 us -> 62.5 us  [across(): return lax.ppermute(value, 'expert', [(p, p ^ bit) for p in range(places)])]
    pallas_call x5 -> x6, Pallas kernels: 88.4 us -> 93.2 us  [mlp(): pl.pallas_call(functools.partial(mlp_kernel, steps, parts, base is not No...]
    all_to_all x4 -> x3, starting transfers between devices: 19.4 us -> 16.8 us  [between_planes(): lax.all_to_all(value.reshape(experts, -1, width), 'expert', split_axis=0,...]
    all_to_all x4 -> x3, waiting for transfers between devices: 79.1 us -> 80 us  [between_planes(): lax.all_to_all(value.reshape(experts, -1, width), 'expert', split_axis=0,...]
  transfers between devices with their start and end apart: 15 -> 14, of which waited for: 9 -> 8; matrix products, arithmetic and copies ran while one was open for 3% -> 4% of each run, Pallas kernels for 17% -> 20%
where the time goes in v3:
time: 396 us; the launch traced here: 392 us
  waiting for transfers between devices  153 us (39%)
  Pallas kernels  104 us (26%)
  blocking collectives  71.5 us (18%)
  starting transfers between devices  25 us (6%)
  matrix products  14 us (4%)
  other arithmetic  12.6 us (3%)
  local copies, waits for them, and re-layouts  10.3 us (3%)
    pallas_call x6, Pallas kernels, mlp(): pl.pallas_call(functools.partial(mlp_kernel, steps, parts, base is not No...  93.2 us
    all_to_all x3, waiting for transfers between devices, between_planes(): lax.all_to_all(value.reshape(experts, -1, width), 'expert', split_axis=0,...  80 us
    ppermute x6, waiting for transfers between devices, across(): return lax.ppermute(value, 'expert', [(p, p ^ bit) for p in range(places)])  62.5 us
    all_to_all x1, blocking collectives, shards(): lax.all_to_all(leaving, 'expert', split_axis=0, concat_axis=0, tiled=True)  55.7 us
    all_to_all x3, starting transfers between devices, between_planes(): lax.all_to_all(value.reshape(experts, -1, width), 'expert', split_axis=0,...  16.8 us
    all_to_all x1, blocking collectives, shards(): lax.all_to_all(result, 'expert', split_axis=0, concat_axis=0, tiled=True)  15.8 us
    ppermute x5, waiting for transfers between devices, other_core(): return lax.ppermute(value, 'seq', [(0, 1), (1, 0)])  10.7 us
    pallas_call x1, Pallas kernels, attention(): pl.pallas_call(functools.partial(attention_kernel, key_tile), grid=(colum...  10.6 us
  transfers between devices with their start and end apart: 14, of which 8 were waited for; matrix products, arithmetic and copies ran while one was open for 4% of the time, Pallas kernels for 20%

profile of v3, /device:TPU:0, one launch (start us, length us, event | category | flops | bytes accessed | tf_op | source)
XLA Modules:
  0.0 392.1 jit_solution(6996666328410976076)
XLA Ops:
  0.7 0.9 copy.29
  1.8 1.4 convert_reduce_fusion.1
  3.8 0.6 broadcast_add_fusion
  4.4 1.2 reduce-window.6
  6.5 0.8 convolution_convert_fusion.1
  7.3 1.4 convolution_convert_fusion
  8.7 1.6 pad_maximum_fusion
  10.3 6.5 %all-to-all-start = ((bf16[4,192,1664]{2,1,0:T(8,128)(2,1)}), bf16[4,192,1664]{2,1,0:T(8,128)(2,1)}, u32[]{:S(2)}, u32[]{:S(2)}) async-start(bf16[4,192,1664]{2,1,0:T(8,128)(2,1)} %pad_maximum_fusion), calls=%async_computation | async-start | bytes 5111808 | tf_op jit(solution)/shard_map/all_to_all | solution.py:184
  17.4 1.5 collective-permute-start
  18.9 0.5 collective-permute-start.6
  19.5 55.5 %all-to-all-done = bf16[4,192,1664]{2,1,0:T(8,128)(2,1)} async-done(((bf16[4,192,1664]{2,1,0:T(8,128)(2,1)}), bf16[4,192,1664]{2,1,0:T(8,128)(2,1)}, u32[]{:S(2)}, u32[]{:S(2)}) %all-to-all-start) | async-done | bytes 2555936 | tf_op jit(solution)/shard_map/all_to_all | solution.py:184
  75.0 3.4 fusion.58
  78.4 1.5 collective-permute-start.3
  79.9 0.5 collective-permute-start.4
  80.4 20.4 %shard_map.77 = (f32[384,1664]{1,0:T(8,128)}, f32[384,1664]{1,0:T(8,128)}) custom-call(bf16[384,1664]{1,0:T(8,128)(2,1)} %bitcast.5.refs_0_, bf16[384,1664]{1,0:T(8,128)(2,1)} %bitcast.7.refs_1_.refs_0_, bf16[1664,1024]{1,0:T(8,128)(2,1)} %bitcast.6.refs_2_, bf16[1664,1024]{1,0:T(8,128)(2,1)} %collective-permute-done.1.refs_3_, ...), custom_call_target="tpu_custom_call" | custom-call | flops 10468982784 | bytes 26411008 | tf_op jit(solution)/shard_map/pallas_call | solution.py:83
  100.8 8.9 %collective-permute-done.3.refs_0_ = bf16[384,1664]{1,0:T(8,128)(2,1)} collective-permute-done((bf16[384,1664]{1,0:T(8,128)(2,1)}, bf16[384,1664]{1,0:T(8,128)(2,1)}, u32[]{:S(2)}, u32[]{:S(2)}) %collective-permute-start.3) | collective-permute-done | bytes 1277984 | tf_op jit(solution)/shard_map/ppermute | solution.py:152
  109.7 25.4 %collective-permute-done.4.refs_1_.refs_0_ = bf16[384,1664]{1,0:T(8,128)(2,1)} collective-permute-done((bf16[384,1664]{1,0:T(8,128)(2,1)}, bf16[384,1664]{1,0:T(8,128)(2,1)}, u32[]{:S(2)}, u32[]{:S(2)}) %collective-permute-start.4) | collective-permute-done | bytes 1277984 | tf_op jit(solution)/shard_map/ppermute | solution.py:152
  135.1 20.3 %shard_map.78 = (f32[384,1664]{1,0:T(8,128)}, f32[384,1664]{1,0:T(8,128)}) custom-call(bf16[384,1664]{1,0:T(8,128)(2,1)} %collective-permute-done.3.refs_0_, bf16[384,1664]{1,0:T(8,128)(2,1)} %collective-permute-done.4.refs_1_.refs_0_, bf16[1664,1024]{1,0:T(8,128)(2,1)} %bitcast.6.refs_2_, bf16[1664,1024]{1,0:T(8,128)(2,1)} %collective-permute-done.1.refs_3_, ...), custom_call_target="tpu_custom_call" | custom-call | flops 10468982784 | bytes 26411008 | tf_op jit(solution)/shard_map/pallas_call | solution.py:83
  155.5 11.0 %collective-permute-done.6.refs_3_ = bf16[1024,1664]{1,0:T(8,128)(2,1)} collective-permute-done((bf16[1024,1664]{1,0:T(8,128)(2,1)}, bf16[1024,1664]{1,0:T(8,128)(2,1)}, u32[]{:S(2)}, u32[]{:S(2)}) %collective-permute-start.6) | collective-permute-done | bytes 3407904 | tf_op jit(solution)/shard_map/ppermute | solution.py:152
  166.5 0.5 collective-permute-start.5
  167.0 10.7 %collective-permute-done.7.refs_4_ = bf16[1024,1664]{1,0:T(8,128)(2,1)} collective-permute-done((bf16[1024,1664]{1,0:T(8,128)(2,1)}, bf16[1024,1664]{1,0:T(8,128)(2,1)}, u32[]{:S(2)}, u32[]{:S(2)}) %collective-permute-start.7) | collective-permute-done | bytes 3407904 | tf_op jit(solution)/shard_map/ppermute | solution.py:155
  177.7 13.1 %shard_map.79 = bf16[384,1664]{1,0:T(8,128)(2,1)} custom-call(bf16[384,1664]{1,0:T(8,128)(2,1)} %collective-permute-done.3.refs_0_, bf16[1664,1024]{1,0:T(8,128)(2,1)} %copy-done.1, bf16[1664,1024]{1,0:T(8,128)(2,1)} %collective-permute-done.5.refs_2_, bf16[1024,1664]{1,0:T(8,128)(2,1)} %collective-permute-done.6.refs_3_, ...), custom_call_target="tpu_custom_call" | custom-call | flops 5234491392 | bytes 20021248 | tf_op jit(solution)/shard_map/pallas_call | solution.py:83
  190.8 1.5 collective-permute-start.8
  192.3 12.9 %shard_map.80 = bf16[384,1664]{1,0:T(8,128)(2,1)} custom-call(bf16[384,1664]{1,0:T(8,128)(2,1)} %collective-permute-done.4.refs_1_.refs_0_, bf16[1664,1024]{1,0:T(8,128)(2,1)} %copy-done.1, bf16[1664,1024]{1,0:T(8,128)(2,1)} %collective-permute-done.5.refs_2_, bf16[1024,1664]{1,0:T(8,128)(2,1)} %collective-permute-done.6.refs_3_, ...), custom_call_target="tpu_custom_call" | custom-call | flops 5234491392 | bytes 20021248 | tf_op jit(solution)/shard_map/pallas_call | solution.py:83
  205.2 13.3 %shard_map.81 = f32[384,1664]{1,0:T(8,128)} custom-call(bf16[384,1664]{1,0:T(8,128)(2,1)} %bitcast.5.refs_0_, bf16[1664,1024]{1,0:T(8,128)(2,1)} %copy-done.1, bf16[1664,1024]{1,0:T(8,128)(2,1)} %collective-permute-done.5.refs_2_, bf16[1024,1664]{1,0:T(8,128)(2,1)} %collective-permute-done.6.refs_3_, bf16[1024,1664]{1,0:T(8,128)(2,1)} %collective-permute-done.7.refs_4_, ...), custom_call_target="tpu_custom_call" | custom-call | flops 5234491392 | bytes 20021248 | tf_op jit(solution)/shard_map/pallas_call | solution.py:83
  218.5 2.7 collective-permute-done.8
  221.1 3.0 add_convert_fusion.1
  224.2 5.1 %all-to-all-start.1 = ((bf16[4,96,1664]{2,1,0:T(8,128)(2,1)}), bf16[4,96,1664]{2,1,0:T(8,128)(2,1)S(1)}, u32[]{:S(2)}, u32[]{:S(2)}) async-start(bf16[4,96,1664]{2,1,0:T(8,128)(2,1)} %bitcast.9), calls=%async_computation.1 | async-start | bytes 2555904 | tf_op jit(solution)/shard_map/all_to_all | solution.py:184
  229.2 1.5 collective-permute-start.9
  230.8 13.3 %shard_map.82 = f32[384,1664]{1,0:T(8,128)} custom-call(bf16[384,1664]{1,0:T(8,128)(2,1)} %bitcast.7.refs_1_.refs_0_, bf16[1664,1024]{1,0:T(8,128)(2,1)} %copy-done.1, bf16[1664,1024]{1,0:T(8,128)(2,1)} %collective-permute-done.5.refs_2_, bf16[1024,1664]{1,0:T(8,128)(2,1)} %collective-permute-done.6.refs_3_, ...), custom_call_target="tpu_custom_call" | custom-call | flops 5234491392 | bytes 20021248 | tf_op jit(solution)/shard_map/pallas_call | solution.py:83
  244.1 14.4 %collective-permute-done.9 = bf16[384,1664]{1,0:T(8,128)(2,1)S(1)} collective-permute-done((bf16[384,1664]{1,0:T(8,128)(2,1)}, bf16[384,1664]{1,0:T(8,128)(2,1)S(1)}, u32[]{:S(2)}, u32[]{:S(2)}) %collective-permute-start.9) | collective-permute-done | bytes 1277984 | tf_op jit(solution)/shard_map/ppermute | solution.py:152
  258.5 3.0 add_convert_fusion
  261.5 5.2 %all-to-all-start.2 = ((bf16[4,96,1664]{2,1,0:T(8,128)(2,1)}), bf16[4,96,1664]{2,1,0:T(8,128)(2,1)S(1)}, u32[]{:S(2)}, u32[]{:S(2)}) async-start(bf16[4,96,1664]{2,1,0:T(8,128)(2,1)} %bitcast.115), calls=%async_computation.2 | async-start | bytes 2555904 | tf_op jit(solution)/shard_map/all_to_all | solution.py:184
  266.9 1.1 select_reduce_fusion.1
  268.1 0.7 convolution_add_fusion.3
  268.8 2.0 convolution_add_fusion.2
  270.8 24.5 %all-to-all-done.2 = bf16[4,96,1664]{2,1,0:T(8,128)(2,1)S(1)} async-done(((bf16[4,96,1664]{2,1,0:T(8,128)(2,1)}), bf16[4,96,1664]{2,1,0:T(8,128)(2,1)S(1)}, u32[]{:S(2)}, u32[]{:S(2)}) %all-to-all-start.2) | async-done | bytes 1277984 | tf_op jit(solution)/shard_map/all_to_all | solution.py:184
  295.3 2.2 convolution_add_fusion.1
  297.5 0.9 convert_reduce_fusion
  299.2 3.7 convolution_convert_fusion.3
  302.9 1.4 select_bitcast_fusion.1
  304.9 55.7 %all_to_all.25 = bf16[16,104,640]{2,1,0:T(8,128)(2,1)S(1)} all-to-all(bf16[16,104,640]{2,1,0:T(8,128)(2,1)S(1)} %bitcast.113), channel_id=1, replica_groups=mesh['group'=1,'expert'=16,'seq'=2] {'expert'}, dimensions={0} | all-to-all | bytes 4259840 | tf_op jit(solution)/shard_map/all_to_all | solution.py:265
  360.7 1.2 copy-done.2
  362.0 0.7 copy.34
  362.7 1.0 copy_bitcast_fusion.q_ref
  363.7 10.6 %shard_map.83 = bf16[104,2048]{1,0:T(8,128)(2,1)S(1)} custom-call(bf16[104,2048]{1,0:T(8,128)(2,1)S(1)} %copy_bitcast_fusion.q_ref, bf16[4096,104]{1,0:T(8,128)(2,1)S(1)} %bitcast.107, bf16[104,4096]{1,0:T(8,128)(2,1)S(1)} %bitcast.108), custom_call_target="tpu_custom_call" | custom-call | flops 3489660928 | bytes 2555904 | tf_op jit(solution)/shard_map/pallas_call | solution.py:123
  374.5 15.8 %all_to_all.26 = bf16[16,104,128]{2,1,0:T(8,128)(2,1)S(1)} all-to-all(bf16[16,104,128]{2,1,0:T(8,128)(2,1)S(1)} %bitcast_bitcast_fusion), channel_id=1, replica_groups=mesh['group'=1,'expert'=16,'seq'=2] {'expert'}, dimensions={0} | all-to-all | bytes 851968 | tf_op jit(solution)/shard_map/all_to_all | solution.py:272
  390.6 1.0 reshape.167
  (79 shorter events, 4.5 us)
Async XLA Ops:
  0.6 266.3 %copy-start = (bf16[1664,4]{0,1:T(4,128)(2,1)S(1)}, bf16[1664,4]{0,1:T(4,128)(2,1)}, u32[]{:S(2)}) copy-start(bf16[1664,4]{0,1:T(4,128)(2,1)} %param.7) | copy-start | bytes 39940
  0.6 2.6 copy-start.4
  3.2 3.3 copy-start.16
  3.6 2.9 copy-start.17
  3.8 2.7 copy-start.6
  6.2 1.1 copy-start.14
  6.5 2.2 copy-start.8
  6.5 2.2 copy-start.11
  10.3 64.6 %all-to-all-start = ((bf16[4,192,1664]{2,1,0:T(8,128)(2,1)}), bf16[4,192,1664]{2,1,0:T(8,128)(2,1)}, u32[]{:S(2)}, u32[]{:S(2)}) async-start(bf16[4,192,1664]{2,1,0:T(8,128)(2,1)} %pad_maximum_fusion), calls=%async_computation | async-start | bytes 5111808 | tf_op jit(solution)/shard_map/all_to_all | solution.py:184
  16.9 63.0 %collective-permute-start.1 = (bf16[1664,1024]{1,0:T(8,128)(2,1)}, bf16[1664,1024]{1,0:T(8,128)(2,1)}, u32[]{:S(2)}, u32[]{:S(2)}) collective-permute-start(bf16[1664,1024]{1,0:T(8,128)(2,1)} %bitcast.6.refs_2_), channel_id=1, source_target_pairs={{0,1},{1,0},{2,3},{3,2},{4,5},{5,4},{6,7},{7,6},{8,9},{9,8},{10,11... | collective-permute-start | bytes 10223624 | tf_op jit(solution)/shard_map/ppermute | solution.py:155
  16.9 63.5 %collective-permute-start.2 = (bf16[1024,1664]{1,0:T(8,128)(2,1)}, bf16[1024,1664]{1,0:T(8,128)(2,1)}, u32[]{:S(2)}, u32[]{:S(2)}) collective-permute-start(bf16[1024,1664]{1,0:T(8,128)(2,1)} %bitcast.8.refs_4_), channel_id=1, source_target_pairs={{0,1},{1,0},{2,3},{3,2},{4,5},{5,4},{6,7},{7,6},{8,9},{9,8},{10,11... | collective-permute-start | bytes 10223624 | tf_op jit(solution)/shard_map/ppermute | solution.py:155
  17.4 138.0 %collective-permute-start = (bf16[1664,1024]{1,0:T(8,128)(2,1)}, bf16[1664,1024]{1,0:T(8,128)(2,1)S(1)}, u32[]{:S(2)}, u32[]{:S(2)}) collective-permute-start(bf16[1664,1024]{1,0:T(8,128)(2,1)} %bitcast.6.refs_2_), channel_id=1, source_target_pairs={{0,2},{2,0},{4,6},{6,4},{8,10},{10,8},{12,14},{14,12},{16,18},{18,... | collective-permute-start | bytes 10223624 | tf_op jit(solution)/shard_map/ppermute | solution.py:152
  18.9 147.6 %collective-permute-start.6 = (bf16[1024,1664]{1,0:T(8,128)(2,1)}, bf16[1024,1664]{1,0:T(8,128)(2,1)}, u32[]{:S(2)}, u32[]{:S(2)}) collective-permute-start(bf16[1024,1664]{1,0:T(8,128)(2,1)} %bitcast.8.refs_4_), channel_id=1, source_target_pairs={{0,2},{2,0},{4,6},{6,4},{8,10},{10,8},{12,14},{14,12},{16,18},{18,... | collective-permute-start | bytes 10223624 | tf_op jit(solution)/shard_map/ppermute | solution.py:152
  78.4 31.3 %collective-permute-start.3 = (bf16[384,1664]{1,0:T(8,128)(2,1)}, bf16[384,1664]{1,0:T(8,128)(2,1)}, u32[]{:S(2)}, u32[]{:S(2)}) collective-permute-start(bf16[384,1664]{1,0:T(8,128)(2,1)} %bitcast.5.refs_0_), channel_id=1, source_target_pairs={{0,4},{2,6},{4,0},{6,2},{8,12},{10,14},{12,8},{14,10},{16,20},{18,... | collective-permute-start | bytes 3833864 | tf_op jit(solution)/shard_map/ppermute | solution.py:152
  79.9 55.2 %collective-permute-start.4 = (bf16[384,1664]{1,0:T(8,128)(2,1)}, bf16[384,1664]{1,0:T(8,128)(2,1)}, u32[]{:S(2)}, u32[]{:S(2)}) collective-permute-start(bf16[384,1664]{1,0:T(8,128)(2,1)} %bitcast.7.refs_1_.refs_0_), channel_id=1, source_target_pairs={{0,4},{2,6},{4,0},{6,2},{8,12},{10,14},{12,8},{14,10},{16,20},{18,... | collective-permute-start | bytes 3833864 | tf_op jit(solution)/shard_map/ppermute | solution.py:152
  155.4 22.3 %copy-start.1 = (bf16[1664,1024]{1,0:T(8,128)(2,1)}, bf16[1664,1024]{1,0:T(8,128)(2,1)S(1)}, u32[]{:S(2)}) copy-start(bf16[1664,1024]{1,0:T(8,128)(2,1)S(1)} %collective-permute-done.refs_1_) | copy-start | bytes 10223620
  166.5 11.2 %collective-permute-start.7 = (bf16[1024,1664]{1,0:T(8,128)(2,1)}, bf16[1024,1664]{1,0:T(8,128)(2,1)}, u32[]{:S(2)}, u32[]{:S(2)}) collective-permute-start(bf16[1024,1664]{1,0:T(8,128)(2,1)} %collective-permute-done.6.refs_3_), channel_id=1, source_target_pairs={{0,1},{1,0},{2,3},{3,2},{4,5},{5,4},{6,7},{7,6},{8,9},{9,8},{10,11... | collective-permute-start | bytes 10223624 | tf_op jit(solution)/shard_map/ppermute | solution.py:155
  166.5 11.2 %collective-permute-start.5 = (bf16[1664,1024]{1,0:T(8,128)(2,1)S(1)}, bf16[1664,1024]{1,0:T(8,128)(2,1)}, u32[]{:S(2)}, u32[]{:S(2)}) collective-permute-start(bf16[1664,1024]{1,0:T(8,128)(2,1)S(1)} %collective-permute-done.refs_1_), channel_id=1, source_target_pairs={{0,1},{1,0},{2,3},{3,2},{4,5},{5,4},{6,7},{7,6},{8,9},{9,8},{10,11... | collective-permute-start | bytes 10223624 | tf_op jit(solution)/shard_map/ppermute | solution.py:155
  190.8 30.3 %collective-permute-start.8 = (bf16[384,1664]{1,0:T(8,128)(2,1)}, bf16[384,1664]{1,0:T(8,128)(2,1)S(1)}, u32[]{:S(2)}, u32[]{:S(2)}) collective-permute-start(bf16[384,1664]{1,0:T(8,128)(2,1)} %shard_map.79), channel_id=1, source_target_pairs={{0,4},{2,6},{4,0},{6,2},{8,12},{10,14},{12,8},{14,10},{16,20},{18,... | collective-permute-start | bytes 3833864 | tf_op jit(solution)/shard_map/ppermute | solution.py:152
  224.2 37.3 %all-to-all-start.1 = ((bf16[4,96,1664]{2,1,0:T(8,128)(2,1)}), bf16[4,96,1664]{2,1,0:T(8,128)(2,1)S(1)}, u32[]{:S(2)}, u32[]{:S(2)}) async-start(bf16[4,96,1664]{2,1,0:T(8,128)(2,1)} %bitcast.9), calls=%async_computation.1 | async-start | bytes 2555904 | tf_op jit(solution)/shard_map/all_to_all | solution.py:184
  229.2 29.2 %collective-permute-start.9 = (bf16[384,1664]{1,0:T(8,128)(2,1)}, bf16[384,1664]{1,0:T(8,128)(2,1)S(1)}, u32[]{:S(2)}, u32[]{:S(2)}) collective-permute-start(bf16[384,1664]{1,0:T(8,128)(2,1)} %shard_map.80), channel_id=1, source_target_pairs={{0,4},{2,6},{4,0},{6,2},{8,12},{10,14},{12,8},{14,10},{16,20},{18,... | collective-permute-start | bytes 3833864 | tf_op jit(solution)/shard_map/ppermute | solution.py:152
  261.5 5.5 %copy-start.5 = (bf16[1,256,1664]{2,1,0:T(8,128)(2,1)S(1)}, bf16[1,256,1664]{2,1,0:T(8,128)(2,1)}, u32[]{:S(2)}) copy-start(bf16[1,256,1664]{2,1,0:T(8,128)(2,1)} %param.6) | copy-start | bytes 2555908
  261.5 33.8 %all-to-all-start.2 = ((bf16[4,96,1664]{2,1,0:T(8,128)(2,1)}), bf16[4,96,1664]{2,1,0:T(8,128)(2,1)S(1)}, u32[]{:S(2)}, u32[]{:S(2)}) async-start(bf16[4,96,1664]{2,1,0:T(8,128)(2,1)} %bitcast.115), calls=%async_computation.2 | async-start | bytes 2555904 | tf_op jit(solution)/shard_map/all_to_all | solution.py:184
  266.7 1.3 copy-start.7
  266.7 1.3 copy-start.9
  266.7 1.3 copy-start.12
  268.8 26.5 %copy-start.10 = (s32[256]{0:T(256)S(1)}, s32[256]{0:T(256)}, u32[]{:S(2)}) copy-start(s32[256]{0:T(256)} %copy-done.8) | copy-start | bytes 3076
  268.8 26.5 %copy-start.13 = (s32[256]{0:T(256)S(1)}, s32[256]{0:T(256)}, u32[]{:S(2)}) copy-start(s32[256]{0:T(256)} %copy-done.11) | copy-start | bytes 3076
  268.8 26.5 %copy-start.15 = (s32[384]{0:T(512)S(1)}, s32[384]{0:T(512)}, u32[]{:S(2)}) copy-start(s32[384]{0:T(512)} %broadcast_add_fusion) | copy-start | bytes 4612
  298.4 4.5 %copy-start.3 = (bf16[256,1664]{1,0:T(8,128)(2,1)}, bf16[256,1664]{1,0:T(8,128)(2,1)S(1)}, u32[]{:S(2)}) copy-start(bf16[256,1664]{1,0:T(8,128)(2,1)S(1)} %get-tuple-element.52) | copy-start | bytes 2555908
  299.1 3.8 collective-permute-start.10
  299.2 3.7 copy-start.18
  360.6 1.4 copy-start.2

commit v4 on v3

--- a/solution.py
+++ b/solution.py
@@ -216,7 +216,9 @@
     far_sum = mlp(far_rows, chip_in, chip_out, None, jnp.float32)
     far_in, near_sum, far_sum = lax.optimization_barrier((far_weights[0], near_sum, far_sum))
     far_core_in = other_core(far_in)
-    far_out, far_sum = lax.optimization_barrier((far_weights[1], far_sum))
+    far_out, far_core_in, far_sum = lax.optimization_barrier(
+        (far_weights[1], far_core_in, far_sum)
+    )
     far_weights = (far_in, far_out)
     far_core_weights = (far_core_in, other_core(far_out))
     next_in, next_out = zip(far_weights, far_core_weights)

time: 396 us -> 393 us (level)
  waiting for transfers between devices: 153 us -> 148 us
    ppermute x5, waiting for transfers between devices: 10.7 us -> 6.38 us  [other_core(): return lax.ppermute(value, 'seq', [(0, 1), (1, 0)])]
  transfers between devices with their start and end apart: 14 -> 14, of which waited for: 8 -> 8; matrix products, arithmetic and copies ran while one was open for 4% -> 4% of each run, Pallas kernels for 20% -> 21%
where the time goes in v4:
time: 393 us; the launch traced here: 389 us
  waiting for transfers between devices  148 us (38%)
  Pallas kernels  104 us (26%)
  blocking collectives  71.5 us (18%)
  starting transfers between devices  25.5 us (6%)
  matrix products  14.1 us (4%)
  other arithmetic  12.6 us (3%)
  local copies, waits for them, and re-layouts  12.1 us (3%)
    pallas_call x6, Pallas kernels, mlp(): pl.pallas_call(functools.partial(mlp_kernel, steps, parts, base is not No...  93.2 us
    all_to_all x3, waiting for transfers between devices, between_planes(): lax.all_to_all(value.reshape(experts, -1, width), 'expert', split_axis=0,...  80.5 us
    ppermute x6, waiting for transfers between devices, across(): return lax.ppermute(value, 'expert', [(p, p ^ bit) for p in range(places)])  60.9 us
    all_to_all x1, blocking collectives, shards(): lax.all_to_all(leaving, 'expert', split_axis=0, concat_axis=0, tiled=True)  55.7 us
    all_to_all x3, starting transfers between devices, between_planes(): lax.all_to_all(value.reshape(experts, -1, width), 'expert', split_axis=0,...  16.8 us
    all_to_all x1, blocking collectives, shards(): lax.all_to_all(result, 'expert', split_axis=0, concat_axis=0, tiled=True)  15.8 us
    pallas_call x1, Pallas kernels, attention(): pl.pallas_call(functools.partial(attention_kernel, key_tile), grid=(colum...  10.6 us
    ppermute x6, starting transfers between devices, across(): return lax.ppermute(value, 'expert', [(p, p ^ bit) for p in range(places)])  8.05 us
  transfers between devices with their start and end apart: 14, of which 8 were waited for; matrix products, arithmetic and copies ran while one was open for 4% of the time, Pallas kernels for 21%

profile of v4, /device:TPU:0, one launch (start us, length us, event | category | flops | bytes accessed | tf_op | source)
XLA Modules:
  0.0 389.0 jit_solution(10162319654646726202)
XLA Ops:
  0.7 0.9 copy.29
  1.8 1.4 convert_reduce_fusion.1
  3.8 0.6 broadcast_add_fusion
  4.4 1.2 reduce-window.6
  6.5 0.8 convolution_convert_fusion.1
  7.3 1.4 convolution_convert_fusion
  8.7 1.7 pad_maximum_fusion
  10.4 6.5 %all-to-all-start = ((bf16[4,192,1664]{2,1,0:T(8,128)(2,1)}), bf16[4,192,1664]{2,1,0:T(8,128)(2,1)}, u32[]{:S(2)}, u32[]{:S(2)}) async-start(bf16[4,192,1664]{2,1,0:T(8,128)(2,1)} %pad_maximum_fusion), calls=%async_computation | async-start | bytes 5111808 | tf_op jit(solution)/shard_map/all_to_all | solution.py:184
  17.5 1.5 collective-permute-start
  18.9 56.0 %all-to-all-done = bf16[4,192,1664]{2,1,0:T(8,128)(2,1)} async-done(((bf16[4,192,1664]{2,1,0:T(8,128)(2,1)}), bf16[4,192,1664]{2,1,0:T(8,128)(2,1)}, u32[]{:S(2)}, u32[]{:S(2)}) %all-to-all-start) | async-done | bytes 2555936 | tf_op jit(solution)/shard_map/all_to_all | solution.py:184
  75.0 3.4 fusion.58
  78.4 1.5 collective-permute-start.3
  79.9 0.5 collective-permute-start.4
  80.4 1.5 collective-permute-start.5
  81.9 20.4 %shard_map.77 = (f32[384,1664]{1,0:T(8,128)}, f32[384,1664]{1,0:T(8,128)}) custom-call(bf16[384,1664]{1,0:T(8,128)(2,1)} %bitcast.5.refs_0_, bf16[384,1664]{1,0:T(8,128)(2,1)} %bitcast.7.refs_1_.refs_0_, bf16[1664,1024]{1,0:T(8,128)(2,1)} %bitcast.6.refs_2_, bf16[1664,1024]{1,0:T(8,128)(2,1)} %collective-permute-done.1.refs_3_, ...), custom_call_target="tpu_custom_call" | custom-call | flops 10468982784 | bytes 26411008 | tf_op jit(solution)/shard_map/pallas_call | solution.py:83
  102.3 7.5 %collective-permute-done.3.refs_0_ = bf16[384,1664]{1,0:T(8,128)(2,1)} collective-permute-done((bf16[384,1664]{1,0:T(8,128)(2,1)}, bf16[384,1664]{1,0:T(8,128)(2,1)}, u32[]{:S(2)}, u32[]{:S(2)}) %collective-permute-start.3) | collective-permute-done | bytes 1277984 | tf_op jit(solution)/shard_map/ppermute | solution.py:152
  109.7 25.4 %collective-permute-done.4.refs_1_.refs_0_ = bf16[384,1664]{1,0:T(8,128)(2,1)} collective-permute-done((bf16[384,1664]{1,0:T(8,128)(2,1)}, bf16[384,1664]{1,0:T(8,128)(2,1)}, u32[]{:S(2)}, u32[]{:S(2)}) %collective-permute-start.4) | collective-permute-done | bytes 1277984 | tf_op jit(solution)/shard_map/ppermute | solution.py:152
  135.1 20.3 %shard_map.78 = (f32[384,1664]{1,0:T(8,128)}, f32[384,1664]{1,0:T(8,128)}) custom-call(bf16[384,1664]{1,0:T(8,128)(2,1)} %collective-permute-done.3.refs_0_, bf16[384,1664]{1,0:T(8,128)(2,1)} %collective-permute-done.4.refs_1_.refs_0_, bf16[1664,1024]{1,0:T(8,128)(2,1)} %bitcast.6.refs_2_, bf16[1664,1024]{1,0:T(8,128)(2,1)} %collective-permute-done.1.refs_3_, ...), custom_call_target="tpu_custom_call" | custom-call | flops 10468982784 | bytes 26411008 | tf_op jit(solution)/shard_map/pallas_call | solution.py:83
  155.5 11.0 %collective-permute-done.5.refs_3_ = bf16[1024,1664]{1,0:T(8,128)(2,1)} collective-permute-done((bf16[1024,1664]{1,0:T(8,128)(2,1)}, bf16[1024,1664]{1,0:T(8,128)(2,1)}, u32[]{:S(2)}, u32[]{:S(2)}) %collective-permute-start.5) | collective-permute-done | bytes 3407904 | tf_op jit(solution)/shard_map/ppermute | solution.py:152
  166.5 1.8 copy-done.2
  168.3 6.4 %collective-permute-done.7.refs_4_ = bf16[1024,1664]{1,0:T(8,128)(2,1)} collective-permute-done((bf16[1024,1664]{1,0:T(8,128)(2,1)}, bf16[1024,1664]{1,0:T(8,128)(2,1)}, u32[]{:S(2)}, u32[]{:S(2)}) %collective-permute-start.7) | collective-permute-done | bytes 3407904 | tf_op jit(solution)/shard_map/ppermute | solution.py:155
  174.7 13.1 %shard_map.79 = bf16[384,1664]{1,0:T(8,128)(2,1)} custom-call(bf16[384,1664]{1,0:T(8,128)(2,1)} %collective-permute-done.3.refs_0_, bf16[1664,1024]{1,0:T(8,128)(2,1)} %copy-done.1, bf16[1664,1024]{1,0:T(8,128)(2,1)} %copy-done.2, bf16[1024,1664]{1,0:T(8,128)(2,1)} %collective-permute-done.5.refs_3_, bf16[1024,1664]{1,0:T(8,128)(2,1)} %collective-permute-done.7.refs_4_, ...), custom_call_target="tpu_custom_call" | custom-call | flops 5234491392 | bytes 20021248 | tf_op jit(solution)/shard_map/pallas_call | solution.py:83
  187.8 1.5 collective-permute-start.8
  189.3 12.8 %shard_map.80 = bf16[384,1664]{1,0:T(8,128)(2,1)} custom-call(bf16[384,1664]{1,0:T(8,128)(2,1)} %collective-permute-done.4.refs_1_.refs_0_, bf16[1664,1024]{1,0:T(8,128)(2,1)} %copy-done.1, bf16[1664,1024]{1,0:T(8,128)(2,1)} %copy-done.2, bf16[1024,1664]{1,0:T(8,128)(2,1)} %collective-permute-done.5.refs_3_, ...), custom_call_target="tpu_custom_call" | custom-call | flops 5234491392 | bytes 20021248 | tf_op jit(solution)/shard_map/pallas_call | solution.py:83
  202.2 13.3 %shard_map.81 = f32[384,1664]{1,0:T(8,128)} custom-call(bf16[384,1664]{1,0:T(8,128)(2,1)} %bitcast.5.refs_0_, bf16[1664,1024]{1,0:T(8,128)(2,1)} %copy-done.1, bf16[1664,1024]{1,0:T(8,128)(2,1)} %copy-done.2, bf16[1024,1664]{1,0:T(8,128)(2,1)} %collective-permute-done.5.refs_3_, bf16[1024,1664]{1,0:T(8,128)(2,1)} %collective-permute-done.7.refs_4_, ...), custom_call_target="tpu_custom_call" | custom-call | flops 5234491392 | bytes 20021248 | tf_op jit(solution)/shard_map/pallas_call | solution.py:83
  215.4 2.7 collective-permute-done.8
  218.1 3.0 add_convert_fusion.1
  221.1 5.1 %all-to-all-start.1 = ((bf16[4,96,1664]{2,1,0:T(8,128)(2,1)}), bf16[4,96,1664]{2,1,0:T(8,128)(2,1)S(1)}, u32[]{:S(2)}, u32[]{:S(2)}) async-start(bf16[4,96,1664]{2,1,0:T(8,128)(2,1)} %bitcast.9), calls=%async_computation.1 | async-start | bytes 2555904 | tf_op jit(solution)/shard_map/all_to_all | solution.py:184
  226.2 1.5 collective-permute-start.9
  227.7 13.3 %shard_map.82 = f32[384,1664]{1,0:T(8,128)} custom-call(bf16[384,1664]{1,0:T(8,128)(2,1)} %bitcast.7.refs_1_.refs_0_, bf16[1664,1024]{1,0:T(8,128)(2,1)} %copy-done.1, bf16[1664,1024]{1,0:T(8,128)(2,1)} %copy-done.2, bf16[1024,1664]{1,0:T(8,128)(2,1)} %collective-permute-done.5.refs_3_, bf16[1024,1664]{1,0:T(8,128)(2,1)} %collective-permute-done.7.refs_4_, ...), custom_call_target="tpu_custom_call" | custom-call | flops 5234491392 | bytes 20021248 | tf_op jit(solution)/shard_map/pallas_call | solution.py:83
  241.0 14.4 %collective-permute-done.9 = bf16[384,1664]{1,0:T(8,128)(2,1)S(1)} collective-permute-done((bf16[384,1664]{1,0:T(8,128)(2,1)}, bf16[384,1664]{1,0:T(8,128)(2,1)S(1)}, u32[]{:S(2)}, u32[]{:S(2)}) %collective-permute-start.9) | collective-permute-done | bytes 1277984 | tf_op jit(solution)/shard_map/ppermute | solution.py:152
  255.4 3.0 add_convert_fusion
  258.4 5.2 %all-to-all-start.2 = ((bf16[4,96,1664]{2,1,0:T(8,128)(2,1)}), bf16[4,96,1664]{2,1,0:T(8,128)(2,1)S(1)}, u32[]{:S(2)}, u32[]{:S(2)}) async-start(bf16[4,96,1664]{2,1,0:T(8,128)(2,1)} %bitcast.115), calls=%async_computation.2 | async-start | bytes 2555904 | tf_op jit(solution)/shard_map/all_to_all | solution.py:184
  263.9 1.1 select_reduce_fusion.1
  265.0 0.7 convolution_add_fusion.3
  265.8 2.0 convolution_add_fusion.2
  267.8 24.5 %all-to-all-done.2 = bf16[4,96,1664]{2,1,0:T(8,128)(2,1)S(1)} async-done(((bf16[4,96,1664]{2,1,0:T(8,128)(2,1)}), bf16[4,96,1664]{2,1,0:T(8,128)(2,1)S(1)}, u32[]{:S(2)}, u32[]{:S(2)}) %all-to-all-start.2) | async-done | bytes 1277984 | tf_op jit(solution)/shard_map/all_to_all | solution.py:184
  292.2 2.2 convolution_add_fusion.1
  294.4 0.9 convert_reduce_fusion
  296.1 3.7 convolution_convert_fusion.3
  299.8 1.4 select_bitcast_fusion.1
  301.8 55.7 %all_to_all.25 = bf16[16,104,640]{2,1,0:T(8,128)(2,1)S(1)} all-to-all(bf16[16,104,640]{2,1,0:T(8,128)(2,1)S(1)} %bitcast.113), channel_id=1, replica_groups=mesh['group'=1,'expert'=16,'seq'=2] {'expert'}, dimensions={0} | all-to-all | bytes 4259840 | tf_op jit(solution)/shard_map/all_to_all | solution.py:267
  357.7 1.2 copy-done.3
  359.0 0.7 copy.34
  359.7 1.0 copy_bitcast_fusion.q_ref
  360.7 10.6 %shard_map.83 = bf16[104,2048]{1,0:T(8,128)(2,1)S(1)} custom-call(bf16[104,2048]{1,0:T(8,128)(2,1)S(1)} %copy_bitcast_fusion.q_ref, bf16[4096,104]{1,0:T(8,128)(2,1)S(1)} %bitcast.107, bf16[104,4096]{1,0:T(8,128)(2,1)S(1)} %bitcast.108), custom_call_target="tpu_custom_call" | custom-call | flops 3489660928 | bytes 2555904 | tf_op jit(solution)/shard_map/pallas_call | solution.py:123
  371.4 15.8 %all_to_all.26 = bf16[16,104,128]{2,1,0:T(8,128)(2,1)S(1)} all-to-all(bf16[16,104,128]{2,1,0:T(8,128)(2,1)S(1)} %bitcast_bitcast_fusion), channel_id=1, replica_groups=mesh['group'=1,'expert'=16,'seq'=2] {'expert'}, dimensions={0} | all-to-all | bytes 851968 | tf_op jit(solution)/shard_map/all_to_all | solution.py:274
  387.6 1.0 reshape.167
  (81 shorter events, 4.6 us)
Async XLA Ops:
  0.6 263.2 %copy-start = (bf16[1664,4]{0,1:T(4,128)(2,1)S(1)}, bf16[1664,4]{0,1:T(4,128)(2,1)}, u32[]{:S(2)}) copy-start(bf16[1664,4]{0,1:T(4,128)(2,1)} %param.7) | copy-start | bytes 39940
  0.6 2.6 copy-start.5
  3.2 3.3 copy-start.17
  3.6 2.9 copy-start.18
  3.8 2.7 copy-start.7
  6.2 1.1 copy-start.15
  6.5 2.2 copy-start.9
  6.5 2.2 copy-start.12
  10.4 64.6 %all-to-all-start = ((bf16[4,192,1664]{2,1,0:T(8,128)(2,1)}), bf16[4,192,1664]{2,1,0:T(8,128)(2,1)}, u32[]{:S(2)}, u32[]{:S(2)}) async-start(bf16[4,192,1664]{2,1,0:T(8,128)(2,1)} %pad_maximum_fusion), calls=%async_computation | async-start | bytes 5111808 | tf_op jit(solution)/shard_map/all_to_all | solution.py:184
  16.9 63.5 %collective-permute-start.1 = (bf16[1664,1024]{1,0:T(8,128)(2,1)}, bf16[1664,1024]{1,0:T(8,128)(2,1)}, u32[]{:S(2)}, u32[]{:S(2)}) collective-permute-start(bf16[1664,1024]{1,0:T(8,128)(2,1)} %bitcast.6.refs_2_), channel_id=1, source_target_pairs={{0,1},{1,0},{2,3},{3,2},{4,5},{5,4},{6,7},{7,6},{8,9},{9,8},{10,11... | collective-permute-start | bytes 10223624 | tf_op jit(solution)/shard_map/ppermute | solution.py:155
  17.0 65.0 %collective-permute-start.2 = (bf16[1024,1664]{1,0:T(8,128)(2,1)}, bf16[1024,1664]{1,0:T(8,128)(2,1)}, u32[]{:S(2)}, u32[]{:S(2)}) collective-permute-start(bf16[1024,1664]{1,0:T(8,128)(2,1)} %bitcast.8.refs_4_), channel_id=1, source_target_pairs={{0,1},{1,0},{2,3},{3,2},{4,5},{5,4},{6,7},{7,6},{8,9},{9,8},{10,11... | collective-permute-start | bytes 10223624 | tf_op jit(solution)/shard_map/ppermute | solution.py:155
  17.5 138.0 %collective-permute-start = (bf16[1664,1024]{1,0:T(8,128)(2,1)}, bf16[1664,1024]{1,0:T(8,128)(2,1)S(1)}, u32[]{:S(2)}, u32[]{:S(2)}) collective-permute-start(bf16[1664,1024]{1,0:T(8,128)(2,1)} %bitcast.6.refs_2_), channel_id=1, source_target_pairs={{0,2},{2,0},{4,6},{6,4},{8,10},{10,8},{12,14},{14,12},{16,18},{18,... | collective-permute-start | bytes 10223624 | tf_op jit(solution)/shard_map/ppermute | solution.py:152
  78.4 31.3 %collective-permute-start.3 = (bf16[384,1664]{1,0:T(8,128)(2,1)}, bf16[384,1664]{1,0:T(8,128)(2,1)}, u32[]{:S(2)}, u32[]{:S(2)}) collective-permute-start(bf16[384,1664]{1,0:T(8,128)(2,1)} %bitcast.5.refs_0_), channel_id=1, source_target_pairs={{0,4},{2,6},{4,0},{6,2},{8,12},{10,14},{12,8},{14,10},{16,20},{18,... | collective-permute-start | bytes 3833864 | tf_op jit(solution)/shard_map/ppermute | solution.py:152
  79.9 55.2 %collective-permute-start.4 = (bf16[384,1664]{1,0:T(8,128)(2,1)}, bf16[384,1664]{1,0:T(8,128)(2,1)}, u32[]{:S(2)}, u32[]{:S(2)}) collective-permute-start(bf16[384,1664]{1,0:T(8,128)(2,1)} %bitcast.7.refs_1_.refs_0_), channel_id=1, source_target_pairs={{0,4},{2,6},{4,0},{6,2},{8,12},{10,14},{12,8},{14,10},{16,20},{18,... | collective-permute-start | bytes 3833864 | tf_op jit(solution)/shard_map/ppermute | solution.py:152
  80.4 86.1 %collective-permute-start.5 = (bf16[1024,1664]{1,0:T(8,128)(2,1)}, bf16[1024,1664]{1,0:T(8,128)(2,1)}, u32[]{:S(2)}, u32[]{:S(2)}) collective-permute-start(bf16[1024,1664]{1,0:T(8,128)(2,1)} %bitcast.8.refs_4_), channel_id=1, source_target_pairs={{0,2},{2,0},{4,6},{6,4},{8,10},{10,8},{12,14},{14,12},{16,18},{18,... | collective-permute-start | bytes 10223624 | tf_op jit(solution)/shard_map/ppermute | solution.py:152
  155.5 19.2 %copy-start.1 = (bf16[1664,1024]{1,0:T(8,128)(2,1)}, bf16[1664,1024]{1,0:T(8,128)(2,1)S(1)}, u32[]{:S(2)}) copy-start(bf16[1664,1024]{1,0:T(8,128)(2,1)S(1)} %collective-permute-done.refs_1_) | copy-start | bytes 10223620
  155.5 11.0 %collective-permute-start.6 = (bf16[1664,1024]{1,0:T(8,128)(2,1)S(1)}, bf16[1664,1024]{1,0:T(8,128)(2,1)S(1)}, u32[]{:S(2)}, u32[]{:S(2)}) collective-permute-start(bf16[1664,1024]{1,0:T(8,128)(2,1)S(1)} %collective-permute-done.refs_1_), channel_id=1, source_target_pairs={{0,1},{1,0},{2,3},{3,2},{4,5},{5,4},{6,7},{7,6},{8,9},{9,8},{10,11... | collective-permute-start | bytes 10223624 | tf_op jit(solution)/shard_map/ppermute | solution.py:155
  166.5 1.8 copy-start.2
  168.3 6.4 %collective-permute-start.7 = (bf16[1024,1664]{1,0:T(8,128)(2,1)}, bf16[1024,1664]{1,0:T(8,128)(2,1)}, u32[]{:S(2)}, u32[]{:S(2)}) collective-permute-start(bf16[1024,1664]{1,0:T(8,128)(2,1)} %collective-permute-done.5.refs_3_), channel_id=1, source_target_pairs={{0,1},{1,0},{2,3},{3,2},{4,5},{5,4},{6,7},{7,6},{8,9},{9,8},{10,11... | collective-permute-start | bytes 10223624 | tf_op jit(solution)/shard_map/ppermute | solution.py:155
  187.8 30.3 %collective-permute-start.8 = (bf16[384,1664]{1,0:T(8,128)(2,1)}, bf16[384,1664]{1,0:T(8,128)(2,1)S(1)}, u32[]{:S(2)}, u32[]{:S(2)}) collective-permute-start(bf16[384,1664]{1,0:T(8,128)(2,1)} %shard_map.79), channel_id=1, source_target_pairs={{0,4},{2,6},{4,0},{6,2},{8,12},{10,14},{12,8},{14,10},{16,20},{18,... | collective-permute-start | bytes 3833864 | tf_op jit(solution)/shard_map/ppermute | solution.py:152
  221.1 37.3 %all-to-all-start.1 = ((bf16[4,96,1664]{2,1,0:T(8,128)(2,1)}), bf16[4,96,1664]{2,1,0:T(8,128)(2,1)S(1)}, u32[]{:S(2)}, u32[]{:S(2)}) async-start(bf16[4,96,1664]{2,1,0:T(8,128)(2,1)} %bitcast.9), calls=%async_computation.1 | async-start | bytes 2555904 | tf_op jit(solution)/shard_map/all_to_all | solution.py:184
  226.2 29.2 %collective-permute-start.9 = (bf16[384,1664]{1,0:T(8,128)(2,1)}, bf16[384,1664]{1,0:T(8,128)(2,1)S(1)}, u32[]{:S(2)}, u32[]{:S(2)}) collective-permute-start(bf16[384,1664]{1,0:T(8,128)(2,1)} %shard_map.80), channel_id=1, source_target_pairs={{0,4},{2,6},{4,0},{6,2},{8,12},{10,14},{12,8},{14,10},{16,20},{18,... | collective-permute-start | bytes 3833864 | tf_op jit(solution)/shard_map/ppermute | solution.py:152
  258.4 5.5 %copy-start.6 = (bf16[1,256,1664]{2,1,0:T(8,128)(2,1)S(1)}, bf16[1,256,1664]{2,1,0:T(8,128)(2,1)}, u32[]{:S(2)}) copy-start(bf16[1,256,1664]{2,1,0:T(8,128)(2,1)} %param.6) | copy-start | bytes 2555908
  258.4 33.8 %all-to-all-start.2 = ((bf16[4,96,1664]{2,1,0:T(8,128)(2,1)}), bf16[4,96,1664]{2,1,0:T(8,128)(2,1)S(1)}, u32[]{:S(2)}, u32[]{:S(2)}) async-start(bf16[4,96,1664]{2,1,0:T(8,128)(2,1)} %bitcast.115), calls=%async_computation.2 | async-start | bytes 2555904 | tf_op jit(solution)/shard_map/all_to_all | solution.py:184
  263.6 1.3 copy-start.8
  263.6 1.3 copy-start.10
  263.7 1.3 copy-start.13
  265.8 26.5 %copy-start.11 = (s32[256]{0:T(256)S(1)}, s32[256]{0:T(256)}, u32[]{:S(2)}) copy-start(s32[256]{0:T(256)} %copy-done.9) | copy-start | bytes 3076
  265.8 26.5 %copy-start.14 = (s32[256]{0:T(256)S(1)}, s32[256]{0:T(256)}, u32[]{:S(2)}) copy-start(s32[256]{0:T(256)} %copy-done.12) | copy-start | bytes 3076
  265.8 26.5 %copy-start.16 = (s32[384]{0:T(512)S(1)}, s32[384]{0:T(512)}, u32[]{:S(2)}) copy-start(s32[384]{0:T(512)} %broadcast_add_fusion) | copy-start | bytes 4612
  295.3 4.5 %copy-start.4 = (bf16[256,1664]{1,0:T(8,128)(2,1)}, bf16[256,1664]{1,0:T(8,128)(2,1)S(1)}, u32[]{:S(2)}) copy-start(bf16[256,1664]{1,0:T(8,128)(2,1)S(1)} %get-tuple-element.54) | copy-start | bytes 2555908
  296.0 3.8 collective-permute-start.10
  296.1 3.7 copy-start.19
  357.6 1.4 copy-start.3
